TPU v7x, 32 devices: a whole 2x2x4 slice. The times are simulated.
32 devices in a mesh: seq: 32 (over z, y, x, core).
Axes of the slice: x: 2, y: 2, z: 4, core: 2. Of those that a mesh axis runs over, the one named last changes fastest.
Arguments:
- queries: bfloat16 [32768, 1024], P('seq'), may hold values from -6 to 6
- keys_values: bfloat16 [32768, 2, 1024], P('seq'), may hold values from -6 to 6
- memory: bfloat16 [128, 64, 256], P('seq'), may hold values from -6 to 6
- block_regions: int32 [512, 4], P('seq'), may hold values from 0 to 127, as said below
- region_slot: int32 [128], replicated, may hold values from 0 to 127, as said below
- grad_out: bfloat16 [32768, 1024], P('seq'), may hold values from -6 to 6
Outputs:
- attended: bfloat16 [32768, 1024], P('seq')
- grad_queries: bfloat16 [32768, 1024], P('seq')
- grad_keys_values: bfloat16 [32768, 2, 1024], P('seq')
Inputs may be any that keep to these rules, and one draw needn't show every extreme that they name: `block_regions`: each block names 4 different regions, and all regions named by the 16 blocks of one device are different. Of the regions named on one device, at most 2 are stored on any one device (the row region_slot[r] of memory lies on device region_slot[r] // 4); in every draw some device stores exactly 2 of the regions named on every device. `region_slot`: A permutation of the regions.
All inputs are finite; a program needn't handle non-finite values.
Results may differ from a plain program's by a relative error of at most 0.0062.
Values may be sent and summed in bfloat16 or wider, within the bound.
A program may use at most 192 MiB of HBM per device.

v0:
```python
import math

import jax
import jax.numpy as jnp
from jax import lax
from jax.sharding import PartitionSpec as P

H = 8
DH = 128
BLK = 64
WIN = 2
MEM = 4


NEG_FILL = -1e30


def with_halo(array, sides, width):
    for axis, dim in sides:
        size, length = (lax.axis_size(axis), array.shape[dim])
        up = [(i, (i + 1) % size) for i in range(size - 1)]
        down = [(j, i) for i, j in up]
        last = lax.slice_in_dim(array, length - width, length, axis=dim)
        leading = lax.slice_in_dim(array, 0, width, axis=dim)
        before = lax.ppermute(last, axis, up)
        after = lax.ppermute(leading, axis, down)
        array = jnp.concatenate([before, array, after], axis=dim)
    return array


def passed_along(array, axis, by):
    length = lax.axis_size(axis)
    pairs = [(i, i + by) for i in range(length) if 0 <= i + by < length]
    return lax.ppermute(array, axis, pairs)


def fetch_memory(memory, block_regions, region_slot):
    region_refs = block_regions.reshape(-1)
    region_count = region_slot.shape[0]
    matches = region_refs[:, None] == jnp.arange(region_count, dtype=jnp.int32)[None, :]
    slot_ids = jnp.sum(jnp.where(matches, region_slot[None, :], 0), axis=1)
    whole_table = lax.all_gather(memory, "seq", axis=0, tiled=True)
    fetched = whole_table[slot_ids]
    return fetched


def per_device(queries, keys_values, memory, block_regions, region_slot, grad_out):
    tok_rows = queries.shape[0]
    blocks = tok_rows // BLK
    devices = lax.axis_size("seq")
    total_blocks = blocks * devices
    first_block = lax.axis_index("seq") * blocks
    window_span = 2 * WIN + 1
    span_rows = window_span * BLK
    score_scale = 1.0 / math.sqrt(DH)
    extended = with_halo(keys_values, (("seq", 0),), WIN * BLK)
    ext_blocks = extended.reshape(blocks + 2 * WIN, BLK, 2, H, DH)
    memory_blocks = fetch_memory(memory, block_regions, region_slot).reshape(
        blocks, MEM * BLK, 2 * DH
    )
    group_size = min(blocks, 8)
    group_count = blocks // group_size

    def stack_window(source, group_first):
        window = lax.dynamic_slice_in_dim(source, group_first, group_size + 2 * WIN, 0)
        stacked = jnp.stack(
            [window[offset : offset + group_size] for offset in range(window_span)], axis=1
        )
        return stacked.reshape((group_size, span_rows) + source.shape[2:])

    def window_inside(group_first):
        neighbour = (
            first_block
            + group_first
            + jnp.arange(group_size, dtype=jnp.int32)[:, None]
            + jnp.arange(window_span, dtype=jnp.int32)[None, :]
            - WIN
        )
        inside = (neighbour >= 0) & (neighbour < total_blocks)
        return jnp.repeat(inside, BLK, axis=1)

    def query_step(running, inputs):
        query_rows, grad_rows, memory_rows, group_first = inputs
        window = stack_window(ext_blocks, group_first)
        win_keys = window[:, :, 0]
        win_values = window[:, :, 1]
        mem_keys = memory_rows[..., :DH]
        mem_values = memory_rows[..., DH:]
        scores = (
            jnp.concatenate(
                [
                    jnp.einsum(
                        "bihe,bjhe->bhij", query_rows, win_keys, preferred_element_type=jnp.float32
                    ),
                    jnp.einsum(
                        "bihe,bje->bhij", query_rows, mem_keys, preferred_element_type=jnp.float32
                    ),
                ],
                axis=-1,
            )
            * score_scale
        )
        valid_keys = jnp.concatenate(
            [window_inside(group_first), jnp.ones((group_size, MEM * BLK), dtype=jnp.bool_)], axis=1
        )
        scores = jnp.where(valid_keys[:, None, None, :], scores, NEG_FILL)
        row_max = jnp.max(scores, axis=-1, keepdims=True)
        exp_scores = jnp.exp(scores - row_max)
        totals = jnp.sum(exp_scores, axis=-1, keepdims=True)
        weights = exp_scores / totals
        weights_low = weights.astype(jnp.bfloat16)
        attended = jnp.einsum(
            "bhij,bjhe->bihe",
            weights_low[..., :span_rows],
            win_values,
            preferred_element_type=jnp.float32,
        )
        attended = attended + jnp.einsum(
            "bhij,bje->bihe",
            weights_low[..., span_rows:],
            mem_values,
            preferred_element_type=jnp.float32,
        )
        grad_probs = jnp.concatenate(
            [
                jnp.einsum(
                    "bihe,bjhe->bhij", grad_rows, win_values, preferred_element_type=jnp.float32
                ),
                jnp.einsum(
                    "bihe,bje->bhij", grad_rows, mem_values, preferred_element_type=jnp.float32
                ),
            ],
            axis=-1,
        )
        row_delta = jnp.sum(weights * grad_probs, axis=-1, keepdims=True)
        grad_low = (weights * (grad_probs - row_delta)).astype(jnp.bfloat16)
        grad_query = jnp.einsum(
            "bhij,bjhe->bihe",
            grad_low[..., :span_rows],
            win_keys,
            preferred_element_type=jnp.float32,
        )
        grad_query = (
            grad_query
            + jnp.einsum(
                "bhij,bje->bihe",
                grad_low[..., span_rows:],
                mem_keys,
                preferred_element_type=jnp.float32,
            )
        ) * score_scale
        log_total = row_max[..., 0] + jnp.log(totals[..., 0])
        row_stats = jnp.stack(
            [jnp.transpose(log_total, (0, 2, 1)), jnp.transpose(row_delta[..., 0], (0, 2, 1))],
            axis=2,
        )
        key_grad = (
            jnp.einsum(
                "bhij,bihe->bjhe",
                grad_low[..., :span_rows],
                query_rows,
                preferred_element_type=jnp.float32,
            )
            * score_scale
        )
        value_grad = jnp.einsum(
            "bhij,bihe->bjhe",
            weights_low[..., :span_rows],
            grad_rows,
            preferred_element_type=jnp.float32,
        )
        pair_grads = jnp.stack([key_grad, value_grad], axis=2).reshape(
            group_size, window_span, BLK, 2, H, DH
        )
        current = lax.dynamic_slice_in_dim(running, group_first, group_size + 2 * WIN, 0)
        for offset in range(window_span):
            current = current.at[offset : offset + group_size].add(pair_grads[:, offset])
        running = lax.dynamic_update_slice_in_dim(running, current, group_first, 0)
        return (
            running,
            (attended.astype(jnp.bfloat16), grad_query.astype(jnp.bfloat16), row_stats),
        )

    inputs = (
        queries.reshape(group_count, group_size, BLK, H, DH),
        grad_out.reshape(group_count, group_size, BLK, H, DH),
        memory_blocks.reshape(group_count, group_size, MEM * BLK, 2 * DH),
        jnp.arange(group_count, dtype=jnp.int32) * group_size,
    )
    starting = jnp.zeros((blocks + 2 * WIN, BLK, 2, H, DH), jnp.float32)
    grads_ext, (attended, grad_query, row_stats) = lax.scan(query_step, starting, inputs)
    from_right = passed_along(grads_ext[:WIN].astype(jnp.bfloat16), "seq", -1).astype(jnp.float32)
    from_left = passed_along(grads_ext[blocks + WIN :].astype(jnp.bfloat16), "seq", 1).astype(
        jnp.float32
    )
    own_grads = grads_ext[WIN : WIN + blocks]
    own_grads = own_grads.at[blocks - WIN :].add(from_right)
    own_grads = own_grads.at[:WIN].add(from_left)
    kv_grads = own_grads.astype(jnp.bfloat16)
    return (
        attended.reshape(tok_rows, H * DH),
        grad_query.reshape(tok_rows, H * DH),
        kv_grads.reshape(tok_rows, 2, H * DH),
    )


def solution(mesh):
    placed = (
        P("seq", None),
        P("seq", None, None),
        P("seq", None, None),
        P("seq", None),
        P(),
        P("seq", None),
    )
    return jax.shard_map(
        per_device,
        mesh=mesh,
        in_specs=placed,
        out_specs=(P("seq", None), P("seq", None), P("seq", None, None)),
        check_vma=False,
    )
```

profile of v0, /device:TPU:1, one launch (start us, length us, event | category | flops | bytes accessed | tf_op | source)
XLA Modules:
  0.0 527.2 jit_solution(9392188394226439717)
XLA Ops:
  23.8 6.4 %collective-permute-done.1 = bf16[128,2,1024]{2,1,0:T(2,128)(2,1)S(1)} collective-permute-done((bf16[128,2,1024]{2,1,0:T(2,128)(2,1)}, bf16[128,2,1024]{2,1,0:T(2,128)(2,1)S(1)}, u32[]{:S(2)}, u32[]{:S(2)}) %collective-permute-start.1) | collective-permute-done | bytes 524320 | tf_op jit(solution)/shard_map/ppermute | solution.py:26
  30.2 19.7 %pad_maximum_fusion.3 = bf16[1280,2,1024]{2,1,0:T(2,128)(2,1)} fusion(bf16[128,2,1024]{2,1,0:T(2,128)(2,1)S(1)} %collective-permute-done.1, bf16[1024,2,1024]{2,1,0:T(2,128)(2,1)} %param.23, bf16[128,2,1024]{2,1,0:T(2,128)(2,1)S(1)} %collective-permute-done), kind=kLoop, calls=%fused_computation.101 | loop fusion | flops 5242880 | bytes 10485760 | tf_op jit(solution)/shard_map/concatenate | solution.py:27
  50.0 9.4 %reshape.401 = bf16[20,64,2,8,128]{4,3,2,1,0:T(8,128)(2,1)} reshape(bf16[1280,2,1024]{2,1,0:T(2,128)(2,1)} %pad_maximum_fusion.3) | data formatting | bytes 10485760 | tf_op jit(solution)/shard_map/reshape | solution.py:57
  59.4 16.7 %all-gather.2.cloned.1.call-done = bf16[128,64,256]{2,1,0:T(8,128)(2,1)} async-done(((bf16[4,64,256]{2,1,0:T(8,128)(2,1)}), bf16[128,64,256]{2,1,0:T(8,128)(2,1)}) %all-gather.2.cloned.1.call-update) | async-done | bytes 4194320 | tf_op jit(solution)/shard_map/all_gather | solution.py:42
  85.5 389.5 %while.24 = (s32[]{:T(128)}, f32[20,64,2,8,128]{4,1,3,0,2:T(8,128)}, bf16[2,8,64,8,128]{4,3,2,1,0:T(8,128)(2,1)}, bf16[2,8,64,8,128]{4,3,2,1,0:T(8,128)(2,1)}, s...) while((s32[]{:T(128)}, ...), condition=%wide.region_5.6_spmd, body=%wide.region_1.5_spmd.sunk | while | flops 3135771904 | bytes 584109952 | solution.py:191
  110.6 7.9 %constant_dynamic-slice_fusion.14 = (bf16[8,64,2,8,128]{4,3,2,1,0:T(8,128)(2,1)S(1)}, bf16[8,64,2,8,128]{4,3,2,1,0:T(8,128)(2,1)S(1)}, bf16[8,64,2,8,128]{4,3,2,...) fusion(bf16[20,64,2,8,128]{4,3,2,1,0:T(8,128)(2,1)} %get-tuple-element.461, ...), kind=kLoop, calls=%fused_computation.87.clone.1 | loop fusion | bytes 20971540 | tf_op jit(solution)/shard_map/while/body/eval_jaxpr/slice | solution.py:67
  129.6 11.9 %copy.127 = bf16[8,5,64,2,8,128]{5,2,1,4,0,3:T(8,128)(2,1)} copy(bf16[8,5,64,2,8,128]{5,2,4,0,3,1:T(8,128)(2,1)} %fusion.105) | data formatting | bytes 20971520 | tf_op jit(solution)/shard_map/while/body/eval_jaxpr/stack | solution.py:66
  141.6 7.3 %fusion.106 = f32[8,8,64,320]{3,2,1,0:T(8,128)} fusion(bf16[8,320,2,8,128]{4,1,3,0,2:T(8,128)(2,1)} %bitcast.245, bf16[1,8,64,8,128]{4,3,2,1,0:T(8,128)(2,1)S(1)} %constant_dynamic-slice_fusion.13), kind=kOutput, calls=%fused_computation.24.clone.1 | convolution fusion | flops 335544320 | bytes 11534336 | tf_op jit(solution)/shard_map/while/body/eval_jaxpr/bihe,bjhe->bhij/dot_general | solution.py:92
  152.6 27.6 %fusion.108 = (f32[8,8,64]{2,1,0:T(8,128)S(1)}, f32[8,8,64,576]{3,2,1,0:T(8,128)}) fusion(f32[8,8,64,256]{3,2,1,0:T(8,128)} %convolution_bitcast_fusion.4, f32[8,8,64,320]{3,2,1,0:T(8,128)} %fusion.106, pred[8,576]{1,0:T(8,128)(4,1)S(1)} %concatenate.50), kind=kOutput, calls=%fused_computation.113.clone.1 | output fusion | flops 11797055 | bytes 18895360 | tf_op jit(solution)/shard_map/while/body/eval_jaxpr/sub | solution.py:108
  187.5 34.1 %fusion.110 = (bf16[8,8,64,576]{3,2,1,0:T(8,128)(2,1)}, bf16[8,8,64,576]{3,2,1,0:T(8,128)(2,1)S(1)}) fusion(f32[8,8,64,576]{3,2,1,0:T(8,128)} %get-tuple-element.410, f32[8,8,64]{2,1,0:T(8,128)S(1)} %get-tuple-element.411, f32[8,8,64,256]{3,2,1,0:T(8,128)} %convolution_bitcast_fusion.5, f32[8,8,64,320]{3,2,1,0:T(8,128)} %fusion.109), kind=kOutput, calls=%fused_computation.100.clone.1 | output fusion | flops 21238336 | bytes 28327936 | tf_op jit(solution)/shard_map/while/body/eval_jaxpr/sub | solution.py:136
  234.8 7.7 %fusion.111 = f32[8,8,128,320]{2,3,1,0:T(8,128)} fusion(bf16[8,8,64,576]{3,2,1,0:T(8,128)(2,1)} %get-tuple-element.413, bf16[1,8,64,8,128]{4,3,2,1,0:T(8,128)(2,1)S(1)} %constant_dynamic-slice_fusion.15), kind=kOutput, calls=%fused_computation.48.clone.1 | convolution fusion | flops 335544320 | bytes 14680064 | tf_op jit(solution)/shard_map/while/body/eval_jaxpr/bhij,bihe->bjhe/dot_general | solution.py:166
  250.7 7.1 %fusion.112 = f32[12,64,2,8,128]{4,1,3,0,2:T(8,128)} fusion(f32[12,64,2,8,128]{4,1,3,0,2:T(8,128)} %constant_dynamic-slice_fusion.12, f32[8,5,64,1,8,128]{5,2,1,4,0,3:T(8,128)} %bitcast.240, f32[8,5,64,1,8,128]{5,2,1,4,0,3:T(8,128)} %bitcast.233, f32[20,64,2,8,128]{4,1,3,0,2:T(8,128)} %get-tuple-element.436, s32[]{:T(128)S(6)} %select_n.50), kind=kLoop, calls=%fused_computation.34.clone.1 | loop fusion | flops 2097152 | bytes 29360132 | tf_op jit(solution)/shard_map/while/body/eval_jaxpr/scatter-add | solution.py:177
  281.6 6.6 %constant_dynamic-update-slice_fusion.2 = f32[20,64,2,8,128]{4,1,3,0,2:T(8,128)} fusion(f32[20,64,2,8,128]{4,1,3,0,2:T(8,128)} %get-tuple-element.436, f32[12,64,2,8,128]{4,1,3,0,2:T(8,128)} %fusion.116, s32[]{:T(128)S(6)} %select_n.49), kind=kLoop, calls=%fused_computation.85.clone.1 | loop fusion | bytes 12582916 | tf_op jit(solution)/shard_map/while/body/eval_jaxpr/dynamic_update_slice | solution.py:178
  290.5 8.1 %constant_dynamic-slice_fusion.14 = (bf16[8,64,2,8,128]{4,3,2,1,0:T(8,128)(2,1)S(1)}, bf16[8,64,2,8,128]{4,3,2,1,0:T(8,128)(2,1)S(1)}, bf16[8,64,2,8,128]{4,3,2,...) fusion(bf16[20,64,2,8,128]{4,3,2,1,0:T(8,128)(2,1)} %get-tuple-element.461, ...), kind=kLoop, calls=%fused_computation.87.clone.1 | loop fusion | bytes 20971540 | tf_op jit(solution)/shard_map/while/body/eval_jaxpr/slice | solution.py:67
  309.7 11.9 %copy.127 = bf16[8,5,64,2,8,128]{5,2,1,4,0,3:T(8,128)(2,1)} copy(bf16[8,5,64,2,8,128]{5,2,4,0,3,1:T(8,128)(2,1)} %fusion.105) | data formatting | bytes 20971520 | tf_op jit(solution)/shard_map/while/body/eval_jaxpr/stack | solution.py:66
  321.7 7.3 %fusion.106 = f32[8,8,64,320]{3,2,1,0:T(8,128)} fusion(bf16[8,320,2,8,128]{4,1,3,0,2:T(8,128)(2,1)} %bitcast.245, bf16[1,8,64,8,128]{4,3,2,1,0:T(8,128)(2,1)S(1)} %constant_dynamic-slice_fusion.13), kind=kOutput, calls=%fused_computation.24.clone.1 | convolution fusion | flops 335544320 | bytes 11534336 | tf_op jit(solution)/shard_map/while/body/eval_jaxpr/bihe,bjhe->bhij/dot_general | solution.py:92
  332.7 27.6 %fusion.108 = (f32[8,8,64]{2,1,0:T(8,128)S(1)}, f32[8,8,64,576]{3,2,1,0:T(8,128)}) fusion(f32[8,8,64,256]{3,2,1,0:T(8,128)} %convolution_bitcast_fusion.4, f32[8,8,64,320]{3,2,1,0:T(8,128)} %fusion.106, pred[8,576]{1,0:T(8,128)(4,1)S(1)} %concatenate.50), kind=kOutput, calls=%fused_computation.113.clone.1 | output fusion | flops 11797055 | bytes 18895360 | tf_op jit(solution)/shard_map/while/body/eval_jaxpr/sub | solution.py:108
  367.6 34.1 %fusion.110 = (bf16[8,8,64,576]{3,2,1,0:T(8,128)(2,1)}, bf16[8,8,64,576]{3,2,1,0:T(8,128)(2,1)S(1)}) fusion(f32[8,8,64,576]{3,2,1,0:T(8,128)} %get-tuple-element.410, f32[8,8,64]{2,1,0:T(8,128)S(1)} %get-tuple-element.411, f32[8,8,64,256]{3,2,1,0:T(8,128)} %convolution_bitcast_fusion.5, f32[8,8,64,320]{3,2,1,0:T(8,128)} %fusion.109), kind=kOutput, calls=%fused_computation.100.clone.1 | output fusion | flops 21238336 | bytes 28327936 | tf_op jit(solution)/shard_map/while/body/eval_jaxpr/sub | solution.py:136
  414.9 7.7 %fusion.111 = f32[8,8,128,320]{2,3,1,0:T(8,128)} fusion(bf16[8,8,64,576]{3,2,1,0:T(8,128)(2,1)} %get-tuple-element.413, bf16[1,8,64,8,128]{4,3,2,1,0:T(8,128)(2,1)S(1)} %constant_dynamic-slice_fusion.15), kind=kOutput, calls=%fused_computation.48.clone.1 | convolution fusion | flops 335544320 | bytes 14680064 | tf_op jit(solution)/shard_map/while/body/eval_jaxpr/bhij,bihe->bjhe/dot_general | solution.py:166
  430.8 7.1 %fusion.112 = f32[12,64,2,8,128]{4,1,3,0,2:T(8,128)} fusion(f32[12,64,2,8,128]{4,1,3,0,2:T(8,128)} %constant_dynamic-slice_fusion.12, f32[8,5,64,1,8,128]{5,2,1,4,0,3:T(8,128)} %bitcast.240, f32[8,5,64,1,8,128]{5,2,1,4,0,3:T(8,128)} %bitcast.233, f32[20,64,2,8,128]{4,1,3,0,2:T(8,128)} %get-tuple-element.436, s32[]{:T(128)S(6)} %select_n.50), kind=kLoop, calls=%fused_computation.34.clone.1 | loop fusion | flops 2097152 | bytes 29360132 | tf_op jit(solution)/shard_map/while/body/eval_jaxpr/scatter-add | solution.py:177
  461.7 6.5 %constant_dynamic-update-slice_fusion.2 = f32[20,64,2,8,128]{4,1,3,0,2:T(8,128)} fusion(f32[20,64,2,8,128]{4,1,3,0,2:T(8,128)} %get-tuple-element.436, f32[12,64,2,8,128]{4,1,3,0,2:T(8,128)} %fusion.116, s32[]{:T(128)S(6)} %select_n.49), kind=kLoop, calls=%fused_computation.85.clone.1 | loop fusion | bytes 12582916 | tf_op jit(solution)/shard_map/while/body/eval_jaxpr/dynamic_update_slice | solution.py:178
  475.0 8.0 %convert.4 = bf16[20,64,2,8,128]{4,1,3,0,2:T(8,128)(2,1)} convert(f32[20,64,2,8,128]{4,1,3,0,2:T(8,128)} %get-tuple-element.265) | non-fusion elementwise | flops 2621440 | bytes 15728640 | tf_op jit(solution)/shard_map/convert.1
  507.8 5.5 %copy.48 = bf16[16,64,2,8,128]{4,3,2,1,0:T(8,128)(2,1)} copy(bf16[16,64,2,8,128]{4,1,3,0,2:T(8,128)(2,1)S(1)} %convert_element_type.41) | data formatting | bytes 8388608 | tf_op jit(solution)/shard_map/convert_element_type | solution.py:199
  513.3 6.9 %reshape.390 = bf16[1024,2,1024]{2,1,0:T(2,128)(2,1)} reshape(bf16[16,64,2,8,128]{4,3,2,1,0:T(8,128)(2,1)} %copy.48) | data formatting | bytes 8388608 | tf_op jit(solution)/shard_map/reshape | solution.py:203
  (168 shorter events, 185.3 us)
Async XLA Ops:
  7.2 14.5 %copy-start.5 = (bf16[1024,1024]{1,0:T(8,128)(2,1)S(1)}, bf16[1024,1024]{1,0:T(8,128)(2,1)}, u32[]{:S(2)}) copy-start(bf16[1024,1024]{1,0:T(8,128)(2,1)} %param.27) | copy-start | bytes 6291460
  7.2 68.9 %all-gather.2.cloned.1.call-start = ((), (), s32[]{:S(2)}) async-start(), calls=%async_computation | async-start | bytes 4325376 | tf_op jit(solution)/shard_map/all_gather | solution.py:42
  7.9 15.7 %copy-start.12 = (s32[128]{0:T(128)S(1)}, s32[128]{0:T(128)}, u32[]{:S(2)}) copy-start(s32[128]{0:T(128)} %param.26) | copy-start | bytes 1540
  10.8 13.0 %collective-permute-start = (bf16[128,2,1024]{2,1,0:T(2,128)(2,1)}, bf16[128,2,1024]{2,1,0:T(2,128)(2,1)S(1)}, u32[]{:S(2)}, u32[]{:S(2)}) collective-permute-start(bf16[128,2,1024]{2,1,0:T(2,128)(2,1)} %get-tuple-element.329), channel_id=1, source_target_pairs={{0,1},{1,2},{2,3},{3,4},{4,5},{5,6},{6,7},{7,8},{8,9},{9,10},{10,1... | collective-permute-start | bytes 1572872 | tf_op jit(solution)/shard_map/ppermute | solution.py:25
  15.3 14.9 %collective-permute-start.1 = (bf16[128,2,1024]{2,1,0:T(2,128)(2,1)}, bf16[128,2,1024]{2,1,0:T(2,128)(2,1)S(1)}, u32[]{:S(2)}, u32[]{:S(2)}) collective-permute-start(bf16[128,2,1024]{2,1,0:T(2,128)(2,1)} %get-tuple-element.330), channel_id=1, source_target_pairs={{1,0},{2,1},{3,2},{4,3},{5,4},{6,5},{7,6},{8,7},{9,8},{10,9},{11,1... | collective-permute-start | bytes 1572872 | tf_op jit(solution)/shard_map/ppermute | solution.py:26
  129.6 11.9 %copy-start.2 = (bf16[2,8,64,8,128]{4,3,2,1,0:T(8,128)(2,1)S(1)}, bf16[2,8,64,8,128]{4,3,2,1,0:T(8,128)(2,1)}, u32[]{:S(2)}) copy-start(bf16[2,8,64,8,128]{4,3,2,1,0:T(8,128)(2,1)} %get-tuple-element.459) | copy-start | bytes 6291460 | tf_op jit(solution)/shard_map/while
  152.5 27.7 %slice-start.3 = ((s8[10485760]{0:T(1024)(128)(4,1)}), s8[4194304]{0:T(1024)(128)(4,1)S(1)}, s32[]{:S(2)}) async-start(s8[10485760]{0:T(1024)(128)(4,1)} %bitcast.246), calls=%async_computation.4 | async-start | bytes 8388608 | tf_op jit(solution)/shard_map/while
  152.5 27.6 %copy-start.3 = (bf16[2,8,64,8,128]{4,3,2,1,0:T(8,128)(2,1)S(1)}, bf16[2,8,64,8,128]{4,3,2,1,0:T(8,128)(2,1)}, u32[]{:S(2)}) copy-start(bf16[2,8,64,8,128]{4,3,2,1,0:T(8,128)(2,1)} %get-tuple-element.463) | copy-start | bytes 6291460 | tf_op jit(solution)/shard_map/while
  152.5 27.7 %slice-start.4 = ((s8[10485760]{0:T(1024)(128)(4,1)}), s8[4194304]{0:T(1024)(128)(4,1)S(1)}, s32[]{:S(2)}) async-start(s8[10485760]{0:T(1024)(128)(4,1)} %bitcast.246), calls=%async_computation.5 | async-start | bytes 8388608 | tf_op jit(solution)/shard_map/while
  152.6 27.7 %slice-start.5 = ((s8[10485760]{0:T(1024)(128)(4,1)}), s8[2097152]{0:T(1024)(128)(4,1)S(1)}, s32[]{:S(2)}) async-start(s8[10485760]{0:T(1024)(128)(4,1)} %bitcast.246), calls=%async_computation.6 | async-start | bytes 4194304 | tf_op jit(solution)/shard_map/while
  234.8 12.5 %slice-start.6 = ((s8[10485760]{0:T(1024)(128)(4,1)}), s8[4194304]{0:T(1024)(128)(4,1)S(1)}, s32[]{:S(2)}) async-start(s8[10485760]{0:T(1024)(128)(4,1)} %bitcast.251), calls=%async_computation.7 | async-start | bytes 8388608 | tf_op jit(solution)/shard_map/while
  234.8 12.5 %slice-start.7 = ((s8[10485760]{0:T(1024)(128)(4,1)}), s8[4194304]{0:T(1024)(128)(4,1)S(1)}, s32[]{:S(2)}) async-start(s8[10485760]{0:T(1024)(128)(4,1)} %bitcast.251), calls=%async_computation.8 | async-start | bytes 8388608 | tf_op jit(solution)/shard_map/while
  247.3 10.4 %slice-start = ((s8[10485760]{0:T(1024)(128)(4,1)}), s8[2097152]{0:T(1024)(128)(4,1)S(1)}, s32[]{:S(2)}) async-start(s8[10485760]{0:T(1024)(128)(4,1)} %bitcast.234), calls=%async_computation.1 | async-start | bytes 4194304 | tf_op jit(solution)/shard_map/while
  309.7 11.9 %copy-start.2 = (bf16[2,8,64,8,128]{4,3,2,1,0:T(8,128)(2,1)S(1)}, bf16[2,8,64,8,128]{4,3,2,1,0:T(8,128)(2,1)}, u32[]{:S(2)}) copy-start(bf16[2,8,64,8,128]{4,3,2,1,0:T(8,128)(2,1)} %get-tuple-element.459) | copy-start | bytes 6291460 | tf_op jit(solution)/shard_map/while
  332.6 27.7 %slice-start.3 = ((s8[10485760]{0:T(1024)(128)(4,1)}), s8[4194304]{0:T(1024)(128)(4,1)S(1)}, s32[]{:S(2)}) async-start(s8[10485760]{0:T(1024)(128)(4,1)} %bitcast.246), calls=%async_computation.4 | async-start | bytes 8388608 | tf_op jit(solution)/shard_map/while
  332.6 27.6 %copy-start.3 = (bf16[2,8,64,8,128]{4,3,2,1,0:T(8,128)(2,1)S(1)}, bf16[2,8,64,8,128]{4,3,2,1,0:T(8,128)(2,1)}, u32[]{:S(2)}) copy-start(bf16[2,8,64,8,128]{4,3,2,1,0:T(8,128)(2,1)} %get-tuple-element.463) | copy-start | bytes 6291460 | tf_op jit(solution)/shard_map/while
  332.7 27.7 %slice-start.4 = ((s8[10485760]{0:T(1024)(128)(4,1)}), s8[4194304]{0:T(1024)(128)(4,1)S(1)}, s32[]{:S(2)}) async-start(s8[10485760]{0:T(1024)(128)(4,1)} %bitcast.246), calls=%async_computation.5 | async-start | bytes 8388608 | tf_op jit(solution)/shard_map/while
  332.7 27.7 %slice-start.5 = ((s8[10485760]{0:T(1024)(128)(4,1)}), s8[2097152]{0:T(1024)(128)(4,1)S(1)}, s32[]{:S(2)}) async-start(s8[10485760]{0:T(1024)(128)(4,1)} %bitcast.246), calls=%async_computation.6 | async-start | bytes 4194304 | tf_op jit(solution)/shard_map/while
  414.9 12.5 %slice-start.6 = ((s8[10485760]{0:T(1024)(128)(4,1)}), s8[4194304]{0:T(1024)(128)(4,1)S(1)}, s32[]{:S(2)}) async-start(s8[10485760]{0:T(1024)(128)(4,1)} %bitcast.251), calls=%async_computation.7 | async-start | bytes 8388608 | tf_op jit(solution)/shard_map/while
  414.9 12.5 %slice-start.7 = ((s8[10485760]{0:T(1024)(128)(4,1)}), s8[4194304]{0:T(1024)(128)(4,1)S(1)}, s32[]{:S(2)}) async-start(s8[10485760]{0:T(1024)(128)(4,1)} %bitcast.251), calls=%async_computation.8 | async-start | bytes 8388608 | tf_op jit(solution)/shard_map/while
  427.4 10.4 %slice-start = ((s8[10485760]{0:T(1024)(128)(4,1)}), s8[2097152]{0:T(1024)(128)(4,1)S(1)}, s32[]{:S(2)}) async-start(s8[10485760]{0:T(1024)(128)(4,1)} %bitcast.234), calls=%async_computation.1 | async-start | bytes 4194304 | tf_op jit(solution)/shard_map/while
  475.0 11.8 %copy-start.1 = (f32[20,64,2,8,128]{4,1,3,0,2:T(8,128)S(1)}, f32[20,64,2,8,128]{4,1,3,0,2:T(8,128)}, u32[]{:S(2)}) copy-start(f32[20,64,2,8,128]{4,1,3,0,2:T(8,128)} %get-tuple-element.265) | copy-start | bytes 31457284
  484.3 13.3 %collective-permute-start.2 = (bf16[2,64,2,8,128]{4,1,3,0,2:T(8,128)(2,1)S(1)}, bf16[2,64,2,8,128]{4,1,3,0,2:T(8,128)(2,1)S(1)}, u32[]{:S(2)}, u32[]{:S(2)}) collective-permute-start(bf16[2,64,2,8,128]{4,1,3,0,2:T(8,128)(2,1)S(1)} %get-tuple-element.328), channel_id=1, source_target_pairs={{1,0},{2,1},{3,2},{4,3},{5,4},{6,5},{7,6},{8,7},{9,8},{10,9},{11,1... | collective-permute-start | bytes 1572872 | tf_op jit(solution)/shard_map/ppermute | solution.py:34
  490.9 10.0 %collective-permute-start.3 = (bf16[2,64,2,8,128]{4,1,3,0,2:T(8,128)(2,1)S(1)}, bf16[2,64,2,8,128]{4,1,3,0,2:T(8,128)(2,1)S(1)}, u32[]{:S(2)}, u32[]{:S(2)}) collective-permute-start(bf16[2,64,2,8,128]{4,1,3,0,2:T(8,128)(2,1)S(1)} %get-tuple-element.327), channel_id=1, source_target_pairs={{0,1},{1,2},{2,3},{3,4},{4,5},{5,6},{6,7},{7,8},{8,9},{9,10},{10,1... | collective-permute-start | bytes 1572872 | tf_op jit(solution)/shard_map/ppermute | solution.py:34
  (20 other events, 107.8 us)
Sparse Core Ops, SparseCore 0:
  10.9 65.1 all-gather.1
where the time goes:
time: 535 us; the launch traced here: 527 us
  other arithmetic  215 us (40%)
  local copies, waits for them, and re-layouts  149 us (28%)
  matrix products  76.2 us (14%)
  loops' own time  34.5 us (6%)
  waiting for transfers between devices  25.8 us (5%)
  between operations  14.4 us (3%)
  starting transfers between devices  12.2 us (2%)
    sub x2, other arithmetic, query_step(): grad_low = (weights * (grad_probs - row_delta)).astype(jnp.bfloat16)  68.2 us
    scatter-add x10, other arithmetic, query_step(): current = current.at[offset:offset + group_size].add(pair_grads[:, offset])  55.3 us
    sub x2, other arithmetic, query_step(): exp_scores = jnp.exp(scores - row_max)  55.1 us
    another operation x1, loops' own time, per_device(): lax.scan(query_step, starting, inputs)  34.5 us
    while x76, local copies, waits for them, and re-layouts  30.8 us
    another operation x4, local copies, waits for them, and re-layouts, stack_window(): jnp.stack([window[offset:offset + group_size] for offset in range(window_...  27.7 us
    concatenate x1, other arithmetic, with_halo(): array = jnp.concatenate([before, array, after], axis=dim)  19.7 us
    all_gather x1, waiting for transfers between devices, fetch_memory(): whole_table = lax.all_gather(memory, 'seq', axis=0, tiled=True)  16.7 us
  transfers between devices with their start and end apart: 5, of which 3 were waited for; matrix products, arithmetic and copies ran while one was open for 9% of the time, Pallas kernels for 0%

commit v1 on v0

v1 whole, which is shorter than its diff:
```python
import functools
import math

import jax
import jax.numpy as jnp
from jax import lax
from jax.experimental import pallas as pl
from jax.experimental.pallas import tpu as pltpu
from jax.sharding import PartitionSpec as P

H = 8
DH = 128
D = H * DH
BLK = 64
WIN = 2
MEM = 4
PAIR = 2 * BLK
HALO = WIN * BLK
SPAN = PAIR + 2 * HALO
NEG_FILL = -1e30
SCALE = 1.0 / math.sqrt(DH)
EXP2_SCALE = SCALE * math.log2(math.e)

NT = (((1,), (1,)), ((), ()))
NN = (((1,), (0,)), ((), ()))
TN = (((0,), (0,)), ((), ()))


def dot(a, b, dims):
    return lax.dot_general(a, b, dims, preferred_element_type=jnp.float32)


def attention_kernel(
    slot_ref, edge_ref, q_ref, do_ref, left_ref, own_ref, right_ref, table_ref,
    att_ref, dq_ref, dkv_ref,
    kv, acc, sems, *, pairs,
):
    step = pl.program_id(0)

    @pl.when(step == 0)
    def _():
        rows = own_ref.shape[0]
        copies = [
            pltpu.make_async_copy(left_ref, kv.at[pl.ds(0, HALO)], sems.at[0]),
            pltpu.make_async_copy(own_ref, kv.at[pl.ds(HALO, rows)], sems.at[1]),
            pltpu.make_async_copy(right_ref, kv.at[pl.ds(HALO + rows, HALO)], sems.at[2]),
        ]
        for copy in copies:
            copy.start()
        acc[pl.ds(0, SPAN - PAIR), :] = jnp.zeros((SPAN - PAIR, 2 * D), jnp.float32)
        for copy in copies:
            copy.wait()

    @pl.when(step < pairs)
    def _():
        base = pl.multiple_of(step * PAIR, PAIR)
        window = pl.ds(base, SPAN)
        row = lax.broadcasted_iota(jnp.int32, (PAIR, PAIR), 0)
        lane = lax.broadcasted_iota(jnp.int32, (PAIR, PAIR), 1)
        no_left = jnp.logical_and(step == 0, edge_ref[0] == 1)
        no_right = jnp.logical_and(step == pairs - 1, edge_ref[1] == 1)
        bias_left = jnp.where(
            jnp.logical_and(jnp.logical_or(row < BLK, lane >= BLK), jnp.logical_not(no_left)),
            0.0, NEG_FILL,
        )
        bias_right = jnp.where(
            jnp.logical_and(jnp.logical_or(row >= BLK, lane < BLK), jnp.logical_not(no_right)),
            0.0, NEG_FILL,
        )

        mem_keys, mem_values = [], []
        for b in range(2):
            parts = [table_ref[slot_ref[(step * 2 + b) * MEM + m]] for m in range(MEM)]
            rows = jnp.concatenate(parts, axis=0)
            mem_keys.append(rows[:, :DH])
            mem_values.append(rows[:, DH:])

        def cols(h):
            return slice(h * DH, (h + 1) * DH)

        def stack(per_head):
            return [
                jnp.concatenate([x[b * BLK : (b + 1) * BLK] for x in per_head], axis=0)
                for b in range(2)
            ]

        def unstack(stacked, h):
            return jnp.concatenate([s[h * BLK : (h + 1) * BLK] for s in stacked], axis=0)

        q = [q_ref[:, cols(h)] for h in range(H)]
        mem_scores = [dot(x, k, NT) for x, k in zip(stack(q), mem_keys)]
        e_win, e_mem, p_win, p_mem, totals, out_win = [], [], [], [], [], []
        for h in range(H):
            sw = dot(q[h], kv[window, cols(h)], NT)
            sw = jnp.concatenate(
                [sw[:, :PAIR] + bias_left, sw[:, PAIR : 2 * PAIR], sw[:, 2 * PAIR :] + bias_right],
                axis=1,
            )
            sm = unstack(mem_scores, h)
            top = jnp.maximum(
                jnp.max(sw, axis=1, keepdims=True), jnp.max(sm, axis=1, keepdims=True)
            )
            ew = jnp.exp2((sw - top) * EXP2_SCALE)
            em = jnp.exp2((sm - top) * EXP2_SCALE)
            totals.append(jnp.sum(ew, axis=1, keepdims=True) + jnp.sum(em, axis=1, keepdims=True))
            e_win.append(ew)
            e_mem.append(em)
            p_win.append(ew.astype(jnp.bfloat16))
            p_mem.append(em.astype(jnp.bfloat16))
            out_win.append(dot(p_win[h], kv[window, slice(D + h * DH, D + (h + 1) * DH)], NN))
        out_mem = [dot(x, v, NN) for x, v in zip(stack(p_mem), mem_values)]
        scaled, deltas = [], []
        for h in range(H):
            inverse = 1.0 / totals[h]
            out = (out_win[h] + unstack(out_mem, h)) * inverse
            att_ref[:, cols(h)] = out.astype(jnp.bfloat16)
            low = (do_ref[:, cols(h)].astype(jnp.float32) * inverse).astype(jnp.bfloat16)
            scaled.append(low)
            deltas.append(jnp.sum(low.astype(jnp.float32) * out, axis=1, keepdims=True))
        mem_probs = [dot(x, v, NT) for x, v in zip(stack(scaled), mem_values)]
        ds_mem, dq_win = [], []
        for h in range(H):
            vcols = slice(D + h * DH, D + (h + 1) * DH)
            pw = dot(scaled[h], kv[window, vcols], NT)
            dsw = (e_win[h] * (pw - deltas[h])).astype(jnp.bfloat16)
            ds_mem.append((e_mem[h] * (unstack(mem_probs, h) - deltas[h])).astype(jnp.bfloat16))
            dq_win.append(dot(dsw, kv[window, cols(h)], NN))
            for columns, low, rows in ((cols(h), dsw, q[h]), (vcols, p_win[h], scaled[h])):
                term = dot(low, rows, TN)
                acc[pl.ds(base, SPAN - PAIR), columns] += term[: SPAN - PAIR]
                acc[pl.ds(base + SPAN - PAIR, PAIR), columns] = term[SPAN - PAIR :]
        dq_mem = [dot(x, k, NN) for x, k in zip(stack(ds_mem), mem_keys)]
        for h in range(H):
            dq_ref[:, cols(h)] = ((dq_win[h] + unstack(dq_mem, h)) * SCALE).astype(jnp.bfloat16)

    done = pl.ds(pl.multiple_of(step * PAIR, PAIR), PAIR)
    dkv_ref[:, :D] = (acc[done, :D] * SCALE).astype(jnp.bfloat16)
    dkv_ref[:, D:] = acc[done, D:].astype(jnp.bfloat16)


def attention(slots, edges, queries, grad_out, left, own, right, table):
    rows = queries.shape[0]
    pairs = rows // PAIR
    steps = pairs + 2 * HALO // PAIR
    ext = rows + 2 * HALO
    by_pair = pl.BlockSpec((PAIR, D), lambda i, *_: (jnp.minimum(i, pairs - 1), 0))
    spec = pltpu.PrefetchScalarGridSpec(
        num_scalar_prefetch=2,
        grid=(steps,),
        in_specs=[
            by_pair,
            by_pair,
            pl.BlockSpec(memory_space=pl.ANY),
            pl.BlockSpec(memory_space=pl.ANY),
            pl.BlockSpec(memory_space=pl.ANY),
            pl.BlockSpec(table.shape, lambda i, *_: (0, 0, 0), pipeline_mode=pl.Buffered(1)),
        ],
        out_specs=[
            by_pair,
            by_pair,
            pl.BlockSpec((PAIR, 2 * D), lambda i, *_: (i, 0)),
        ],
        scratch_shapes=[
            pltpu.VMEM((ext, 2 * D), jnp.bfloat16),
            pltpu.VMEM((ext, 2 * D), jnp.float32),
            pltpu.SemaphoreType.DMA((3,)),
        ],
    )
    return pl.pallas_call(
        functools.partial(attention_kernel, pairs=pairs),
        grid_spec=spec,
        out_shape=[
            jax.ShapeDtypeStruct((rows, D), jnp.bfloat16),
            jax.ShapeDtypeStruct((rows, D), jnp.bfloat16),
            jax.ShapeDtypeStruct((ext, 2 * D), jnp.bfloat16),
        ],
        compiler_params=pltpu.CompilerParams(vmem_limit_bytes=56 * 2**20),
        name="attention",
    )(slots, edges, queries, grad_out, left, own, right, table)


def per_device(queries, keys_values, memory, block_regions, region_slot, grad_out):
    rows = queries.shape[0]
    size = lax.axis_size("seq")
    me = lax.axis_index("seq")
    up = [(i, i + 1) for i in range(size - 1)]
    down = [(j, i) for i, j in up]
    left = lax.ppermute(keys_values[rows - HALO :].reshape(HALO, 2 * D), "seq", up)
    right = lax.ppermute(keys_values[:HALO].reshape(HALO, 2 * D), "seq", down)
    table = lax.all_gather(memory, "seq", axis=0, tiled=True)
    slots = region_slot[block_regions.reshape(-1)]
    edges = jnp.stack([me == 0, me == size - 1]).astype(jnp.int32)
    own = keys_values.reshape(rows, 2 * D)
    attended, grad_queries, grads = attention(
        slots, edges, queries, grad_out, left, own, right, table
    )
    from_right = lax.ppermute(grads[:HALO], "seq", down)
    from_left = lax.ppermute(grads[HALO + rows :], "seq", up)
    kept = grads[HALO : HALO + rows].astype(jnp.float32)
    kept = jnp.concatenate(
        [
            kept[:HALO] + from_left.astype(jnp.float32),
            kept[HALO : rows - HALO],
            kept[rows - HALO :] + from_right.astype(jnp.float32),
        ],
        axis=0,
    )
    return attended, grad_queries, kept.astype(jnp.bfloat16).reshape(rows, 2, D)


def solution(mesh):
    placed = (
        P("seq", None),
        P("seq", None, None),
        P("seq", None, None),
        P("seq", None),
        P(),
        P("seq", None),
    )
    return jax.shard_map(
        per_device,
        mesh=mesh,
        in_specs=placed,
        out_specs=(P("seq", None), P("seq", None), P("seq", None, None)),
        check_vma=False,
    )
```

time: 535 us -> 160 us (0.30); the launches traced: 527 us -> 159 us
  other arithmetic: 215 us -> 14.2 us
  local copies, waits for them, and re-layouts: 149 us -> 22.1 us
  matrix products: 76.2 us -> 0 us
  Pallas kernels: 0 us -> 40.5 us
  loops' own time: 34.5 us -> 0 us
  waiting for transfers between devices: 25.8 us -> 56.8 us
    sub x4 -> x0, other arithmetic: 123 us -> none  [the longest x2 68.2 us: query_step(): grad_low = (weights * (grad_probs - row_delta)).astype(jnp.bfloat16)]
    dot_general x20 -> x0, matrix products: 76.2 us -> none  [the longest x2 15.4 us: query_step(): jnp.einsum('bhij,bihe->bjhe', weights_low[..., :span_rows], grad_rows, pr...]
    scatter-add x12 -> x0, other arithmetic: 58.9 us -> none  [the longest x10 55.3 us: query_step(): current = current.at[offset:offset + group_size].add(pair_grads[:, offset])]
    pallas_call x0 -> x1, Pallas kernels: none -> 40.5 us  [attention(): pl.pallas_call(functools.partial(attention_kernel, pairs=pairs), grid_spe...]
    another operation x1 -> x0, loops' own time: 34.5 us -> none  [per_device(): lax.scan(query_step, starting, inputs)]
    while x76 -> x0, local copies, waits for them, and re-layouts: 30.8 us -> none
    all_gather x1, waiting for transfers between devices: 16.7 us -> 46.7 us  [per_device(): table = lax.all_gather(memory, 'seq', axis=0, tiled=True)]
    another operation x4 -> x0, local copies, waits for them, and re-layouts: 27.7 us -> none  [stack_window(): jnp.stack([window[offset:offset + group_size] for offset in range(window_...]
  transfers between devices with their start and end apart: 5 -> 5, of which waited for: 3 -> 3; matrix products, arithmetic and copies ran while one was open for 9% -> 11% of each run, Pallas kernels for 0% -> 0%
where the time goes in v1:
time: 160 us; the launch traced here: 159 us
  waiting for transfers between devices  56.8 us (36%)
  Pallas kernels  40.5 us (25%)
  local copies, waits for them, and re-layouts  22.1 us (14%)
  other arithmetic  14.2 us (9%)
  between operations  14.2 us (9%)
  starting transfers between devices  11.6 us (7%)
    all_gather x1, waiting for transfers between devices, per_device(): table = lax.all_gather(memory, 'seq', axis=0, tiled=True)  46.7 us
    pallas_call x1, Pallas kernels, attention(): pl.pallas_call(functools.partial(attention_kernel, pairs=pairs), grid_spe...  40.5 us
    concatenate x3, local copies, waits for them, and re-layouts, per_device(): jnp.concatenate([kept[:HALO] + from_left.astype(jnp.float32), kept[HALO:r...  8.4 us
    concatenate x1, other arithmetic, per_device(): jnp.concatenate([kept[:HALO] + from_left.astype(jnp.float32), kept[HALO:r...  7.79 us
    unnamed x14, local copies, waits for them, and re-layouts  5.98 us
    ppermute x1, waiting for transfers between devices, per_device(): right = lax.ppermute(keys_values[:HALO].reshape(HALO, 2 * D), 'seq', down)  4.84 us
    ppermute x1, waiting for transfers between devices, per_device(): from_right = lax.ppermute(grads[:HALO], 'seq', down)  4.54 us
    ppermute x1, starting transfers between devices, per_device(): lax.ppermute(keys_values[rows - HALO:].reshape(HALO, 2 * D), 'seq', up)  4.51 us
  transfers between devices with their start and end apart: 5, of which 3 were waited for; matrix products, arithmetic and copies ran while one was open for 11% of the time, Pallas kernels for 0%

profile of v1, /device:TPU:1, one launch (start us, length us, event | category | flops | bytes accessed | tf_op | source)
XLA Modules:
  0.0 159.4 jit_solution(10450881588532161082)
XLA Ops:
  7.2 0.7 all-gather.2.cloned.1.call-update
  7.9 1.9 %fusion.4 = (bf16[128,2,1024]{2,1,0:T(2,128)(2,1)S(1)}, bf16[128,2,1024]{2,1,0:T(2,128)(2,1)S(1)}) fusion(bf16[1024,2,1024]{2,1,0:T(2,128)(2,1)} %param.7), kind=kLoop, calls=%fused_computation.12 | loop fusion | bytes 2097152 | tf_op jit(solution)/shard_map/slice | solution.py:189
  9.9 0.1 copy.12
  10.0 4.5 %collective-permute-start = (bf16[128,2048]{1,0:T(8,128)(2,1)S(1)}, bf16[128,2048]{1,0:T(8,128)(2,1)S(1)}, u32[]{:S(2)}, u32[]{:S(2)}) collective-permute-start(bf16[128,2048]{1,0:T(8,128)(2,1)S(1)} %bitcast.14), channel_id=1, source_target_pairs={{0,1},{1,2},{2,3},{3,4},{4,5},{5,6},{6,7},{7,8},{8,9},{9,10},{10,1... | collective-permute-start | bytes 1572872 | tf_op jit(solution)/shard_map/ppermute | solution.py:188
  14.5 0.1 copy.14
  14.6 1.9 %collective-permute-start.1 = (bf16[128,2048]{1,0:T(8,128)(2,1)S(1)}, bf16[128,2048]{1,0:T(8,128)(2,1)S(1)}, u32[]{:S(2)}, u32[]{:S(2)}) collective-permute-start(bf16[128,2048]{1,0:T(8,128)(2,1)S(1)} %bitcast.15), channel_id=1, source_target_pairs={{1,0},{2,1},{3,2},{4,3},{5,4},{6,5},{7,6},{8,7},{9,8},{10,9},{11,1... | collective-permute-start | bytes 1572872 | tf_op jit(solution)/shard_map/ppermute | solution.py:189
  16.6 0.1 reshape.53
  16.7 5.6 %copy.13 = bf16[128,8,2,1024]{3,1,2,0:T(8,128)(2,1)} copy(bf16[128,8,2,1024]{3,2,1,0:T(2,128)(2,1)} %bitcast.11) | data formatting | bytes 8388608
  22.4 1.3 gather_fusion
  23.7 0.7 add_convert_fusion.edge_ref
  24.4 4.8 %collective-permute-done.1.right_ref = bf16[128,2048]{1,0:T(8,128)(2,1)S(1)} collective-permute-done((bf16[128,2048]{1,0:T(8,128)(2,1)S(1)}, bf16[128,2048]{1,0:T(8,128)(2,1)S(1)}, u32[]{:S(2)}, u32[]{:S(2)}) %collective-permute-start.1) | collective-permute-done | bytes 524320 | tf_op jit(solution)/shard_map/ppermute | solution.py:189
  29.2 46.7 %all-gather.2.cloned.1.call-done.table_ref = bf16[128,64,256]{2,1,0:T(8,128)(2,1)} async-done(((bf16[4,64,256]{2,1,0:T(8,128)(2,1)}), bf16[128,64,256]{2,1,0:T(8,128)(2,1)}) %all-gather.2.cloned.1.call-update) | async-done | bytes 4194320 | tf_op jit(solution)/shard_map/all_gather | solution.py:190
  75.9 40.5 %attention.1 = (bf16[1024,1024]{1,0:T(8,128)(2,1)}, bf16[1024,1024]{1,0:T(8,128)(2,1)}, bf16[1280,2048]{1,0:T(8,128)(2,1)}) custom-call(s32[64]{0:T(128)} %gather_fusion, s32[2]{0:T(128)} %add_convert_fusion.edge_ref, bf16[1024,1024]{1,0:T(8,128)(2,1)} %q_ref.1, bf16[1024,1024]{1,0:T(8,128)(2,1)} %do_ref.1, bf16[128,2048]{1,0:T(8,128)(2,1)} %copy-done.2, ...), custom_call_target="tpu_custom_call" | custom-call | tf_op jit(solution)/shard_map/attention/pallas_call | solution.py:169
  116.4 2.3 %fusion.3 = (bf16[128,2048]{1,0:T(8,128)(2,1)}, bf16[128,2048]{1,0:T(8,128)(2,1)}) fusion(bf16[1280,2048]{1,0:T(8,128)(2,1)} %get-tuple-element.8), kind=kLoop, calls=%fused_computation.11 | loop fusion | bytes 2097152 | tf_op jit(solution)/shard_map/slice | solution.py:198
  118.7 2.1 %slice.31 = bf16[768,2048]{1,0:T(8,128)(2,1)S(1)} slice(bf16[1280,2048]{1,0:T(8,128)(2,1)} %get-tuple-element.8), slice={[256:1024], [0:2048]} | slice | bytes 6291456 | tf_op jit(solution)/shard_map/slice | solution.py:203
  120.9 3.0 %collective-permute-start.2 = (bf16[128,2048]{1,0:T(8,128)(2,1)}, bf16[128,2048]{1,0:T(8,128)(2,1)}, u32[]{:S(2)}, u32[]{:S(2)}) collective-permute-start(bf16[128,2048]{1,0:T(8,128)(2,1)} %get-tuple-element.11), channel_id=1, source_target_pairs={{0,1},{1,2},{2,3},{3,4},{4,5},{5,6},{6,7},{7,8},{8,9},{9,10},{10,1... | collective-permute-start | bytes 1572872 | tf_op jit(solution)/shard_map/ppermute | solution.py:198
  123.9 2.1 %collective-permute-start.3 = (bf16[128,2048]{1,0:T(8,128)(2,1)}, bf16[128,2048]{1,0:T(8,128)(2,1)}, u32[]{:S(2)}, u32[]{:S(2)}) collective-permute-start(bf16[128,2048]{1,0:T(8,128)(2,1)} %get-tuple-element.12), channel_id=1, source_target_pairs={{1,0},{2,1},{3,2},{4,3},{5,4},{6,5},{7,6},{8,7},{9,8},{10,9},{11,1... | collective-permute-start | bytes 1572872 | tf_op jit(solution)/shard_map/ppermute | solution.py:197
  126.0 3.9 %concatenate.12 = bf16[768,2,1024]{2,1,0:T(2,128)(2,1)} reshape(bf16[768,2048]{1,0:T(8,128)(2,1)S(1)} %slice.31) | data formatting | bytes 6291456 | tf_op jit(solution)/shard_map/concatenate | solution.py:200
  129.9 3.3 %slice_convert_fusion = f32[1024,2048]{1,0:T(8,128)S(1)} fusion(bf16[1280,2048]{1,0:T(8,128)(2,1)} %get-tuple-element.8), kind=kLoop, calls=%fused_computation.2 | loop fusion | flops 2097152 | bytes 12582912 | tf_op jit(solution)/shard_map/convert_element_type | solution.py:199
  133.2 4.5 %collective-permute-done.3 = bf16[128,2048]{1,0:T(8,128)(2,1)} collective-permute-done((bf16[128,2048]{1,0:T(8,128)(2,1)}, bf16[128,2048]{1,0:T(8,128)(2,1)}, u32[]{:S(2)}, u32[]{:S(2)}) %collective-permute-start.3) | collective-permute-done | bytes 524320 | tf_op jit(solution)/shard_map/ppermute | solution.py:197
  137.8 2.5 %fusion.1 = (bf16[128,2048]{1,0:T(8,128)(2,1)}, bf16[128,2048]{1,0:T(8,128)(2,1)}) fusion(f32[1024,2048]{1,0:T(8,128)S(1)} %slice_convert_fusion, bf16[128,2048]{1,0:T(8,128)(2,1)} %collective-permute-done.2, bf16[128,2048]{1,0:T(8,128)(2,1)} %collective-permute-done.3), kind=kLoop, calls=%fused_computation.6 | loop fusion | flops 1572864 | bytes 4194304 | tf_op jit(solution)/shard_map/convert.6
  140.3 2.3 %concatenate.13 = bf16[128,2,1024]{2,1,0:T(2,128)(2,1)} reshape(bf16[128,2048]{1,0:T(8,128)(2,1)} %get-tuple-element.10) | data formatting | bytes 1048576 | tf_op jit(solution)/shard_map/concatenate | solution.py:200
  142.5 2.2 %concatenate.11 = bf16[128,2,1024]{2,1,0:T(2,128)(2,1)} reshape(bf16[128,2048]{1,0:T(8,128)(2,1)} %get-tuple-element.9) | data formatting | bytes 1048576 | tf_op jit(solution)/shard_map/concatenate | solution.py:200
  144.7 7.8 %pad_maximum_fusion = bf16[1024,2,1024]{2,1,0:T(2,128)(2,1)} fusion(bf16[128,2,1024]{2,1,0:T(2,128)(2,1)} %concatenate.13, bf16[768,2,1024]{2,1,0:T(2,128)(2,1)S(1)} %copy-done.1, bf16[128,2,1024]{2,1,0:T(2,128)(2,1)} %concatenate.11), kind=kLoop, calls=%fused_computation.1 | loop fusion | flops 4194304 | bytes 8388608 | tf_op jit(solution)/shard_map/concatenate | solution.py:200
  (16 shorter events, 0.2 us)
Async XLA Ops:
  7.2 15.2 %copy-start = (s32[128]{0:T(128)S(1)}, s32[128]{0:T(128)}, u32[]{:S(2)}) copy-start(s32[128]{0:T(128)} %param.10) | copy-start | bytes 1540
  7.2 9.4 %copy-start.4 = (s32[16,4]{0,1:T(4,128)S(1)}, s32[16,4]{0,1:T(4,128)}, u32[]{:S(2)}) copy-start(s32[16,4]{0,1:T(4,128)} %param.9) | copy-start | bytes 772
  7.2 68.7 %all-gather.2.cloned.1.call-start = ((), (), s32[]{:S(2)}) async-start(), calls=%async_computation | async-start | bytes 4325376 | tf_op jit(solution)/shard_map/all_gather | solution.py:190
  10.0 14.4 %collective-permute-start = (bf16[128,2048]{1,0:T(8,128)(2,1)S(1)}, bf16[128,2048]{1,0:T(8,128)(2,1)S(1)}, u32[]{:S(2)}, u32[]{:S(2)}) collective-permute-start(bf16[128,2048]{1,0:T(8,128)(2,1)S(1)} %bitcast.14), channel_id=1, source_target_pairs={{0,1},{1,2},{2,3},{3,4},{4,5},{5,6},{6,7},{7,8},{8,9},{9,10},{10,1... | collective-permute-start | bytes 1572872 | tf_op jit(solution)/shard_map/ppermute | solution.py:188
  14.6 14.6 %collective-permute-start.1 = (bf16[128,2048]{1,0:T(8,128)(2,1)S(1)}, bf16[128,2048]{1,0:T(8,128)(2,1)S(1)}, u32[]{:S(2)}, u32[]{:S(2)}) collective-permute-start(bf16[128,2048]{1,0:T(8,128)(2,1)S(1)} %bitcast.15), channel_id=1, source_target_pairs={{1,0},{2,1},{3,2},{4,3},{5,4},{6,5},{7,6},{8,7},{9,8},{10,9},{11,1... | collective-permute-start | bytes 1572872 | tf_op jit(solution)/shard_map/ppermute | solution.py:189
  24.4 51.6 %copy-start.2 = (bf16[128,2048]{1,0:T(8,128)(2,1)}, bf16[128,2048]{1,0:T(8,128)(2,1)S(1)}, u32[]{:S(2)}) copy-start(bf16[128,2048]{1,0:T(8,128)(2,1)S(1)} %collective-permute-done.left_ref) | copy-start | bytes 1572868
  29.2 46.7 %copy-start.3 = (bf16[128,2048]{1,0:T(8,128)(2,1)}, bf16[128,2048]{1,0:T(8,128)(2,1)S(1)}, u32[]{:S(2)}) copy-start(bf16[128,2048]{1,0:T(8,128)(2,1)S(1)} %collective-permute-done.1.right_ref) | copy-start | bytes 1572868
  120.9 12.4 %collective-permute-start.2 = (bf16[128,2048]{1,0:T(8,128)(2,1)}, bf16[128,2048]{1,0:T(8,128)(2,1)}, u32[]{:S(2)}, u32[]{:S(2)}) collective-permute-start(bf16[128,2048]{1,0:T(8,128)(2,1)} %get-tuple-element.11), channel_id=1, source_target_pairs={{0,1},{1,2},{2,3},{3,4},{4,5},{5,6},{6,7},{7,8},{8,9},{9,10},{10,1... | collective-permute-start | bytes 1572872 | tf_op jit(solution)/shard_map/ppermute | solution.py:198
  123.9 13.9 %collective-permute-start.3 = (bf16[128,2048]{1,0:T(8,128)(2,1)}, bf16[128,2048]{1,0:T(8,128)(2,1)}, u32[]{:S(2)}, u32[]{:S(2)}) collective-permute-start(bf16[128,2048]{1,0:T(8,128)(2,1)} %get-tuple-element.12), channel_id=1, source_target_pairs={{1,0},{2,1},{3,2},{4,3},{5,4},{6,5},{7,6},{8,7},{9,8},{10,9},{11,1... | collective-permute-start | bytes 1572872 | tf_op jit(solution)/shard_map/ppermute | solution.py:197
  133.2 11.5 %copy-start.1 = (bf16[768,2,1024]{2,1,0:T(2,128)(2,1)S(1)}, bf16[768,2,1024]{2,1,0:T(2,128)(2,1)}, u32[]{:S(2)}) copy-start(bf16[768,2,1024]{2,1,0:T(2,128)(2,1)} %concatenate.12) | copy-start | bytes 9437188
Sparse Core Ops, SparseCore 0:
  10.9 64.9 all-gather.1

commit v2 on v1

--- a/solution.py
+++ b/solution.py
@@ -21,6 +21,8 @@
 SCALE = 1.0 / math.sqrt(DH)
 EXP2_SCALE = SCALE * math.log2(math.e)
 
+MESH = pl.DeviceIdType.MESH
+
 NT = (((1,), (1,)), ((), ()))
 NN = (((1,), (0,)), ((), ()))
 TN = (((0,), (0,)), ((), ()))
@@ -30,9 +32,141 @@
     return lax.dot_general(a, b, dims, preferred_element_type=jnp.float32)
 
 
+def flipped(number, mask):
+    for bit in (1, 2, 4, 8, 16):
+        if mask & bit:
+            number = number + bit - 2 * bit * (number // bit % 2)
+    return number
+
+
+CORE, X, Y, Z, ZZ = 1, 2, 4, 8, 24
+COLUMN = (0, Z, ZZ, Z ^ ZZ)
+
+
+def gather_steps():
+    steps = [(0, None, (Z, ZZ, X, Y, CORE))]
+    steps += [(Z, None, (X, Y, CORE)), (ZZ, None, (Z, X, Y, CORE))]
+    steps += [(X, None, ()), (Y, None, ()), (Z ^ ZZ, None, (X, Y, CORE))]
+    steps += [(side ^ k, None, ()) for k in COLUMN[1:] for side in (X, Y)]
+    steps += [(X ^ Y ^ k, half, (CORE,)) for k in COLUMN for half in (0, 1)]
+    return steps
+
+
+def sends():
+    groups = []
+    for block, half, partners in gather_steps():
+        group = [(block, half, partner) for partner in partners]
+        if block in [X ^ k for k in COLUMN]:
+            group = [(block, 0, Y), (block, None, CORE)]
+        if block in [Y ^ k for k in COLUMN]:
+            group = [(block, 1, X), (block, None, CORE)]
+        groups.append((block, half, group))
+    return groups
+
+
+def exchange_kernel(mem_ref, own_ref, table_ref, left_ref, right_ref, local_sem, send_sems, recv_sems, halo_sems, *, size, gather):
+    me = lax.axis_index("seq")
+    after, before = lax.rem(me + 1, size), lax.rem(me + size - 1, size)
+    masks = (CORE, X, Y, Z, ZZ) if gather else ()
+    barrier = pltpu.get_barrier_semaphore()
+    partners = [flipped(me, mask) for mask in masks] + [after, before]
+    for partner in partners:
+        pl.semaphore_signal(barrier, inc=1, device_id=(partner,), device_id_type=MESH)
+    pl.semaphore_wait(barrier, len(partners))
+
+    rows = own_ref.shape[0]
+    halos = [
+        pltpu.make_async_remote_copy(
+            src_ref=own_ref.at[pl.ds(start, HALO)], dst_ref=dst,
+            send_sem=halo_sems.at[2 * i], recv_sem=halo_sems.at[2 * i + 1],
+            device_id=(target,), device_id_type=MESH,
+        )
+        for i, (start, dst, target) in enumerate(
+            ((rows - HALO, left_ref, after), (0, right_ref, before))
+        )
+    ]
+    if not gather:
+        for halo in halos:
+            halo.start()
+        for halo in halos:
+            halo.wait()
+        return
+    blocks = mem_ref.shape[0]
+
+    def part(half):
+        return (0, blocks) if half is None else (half * (blocks // 2), blocks // 2)
+
+    def slot(block, half):
+        start, length = part(half)
+        return table_ref.at[pl.ds(flipped(me, block) * blocks + start, length)]
+
+    def copy(block, half, partner, number):
+        start, length = part(half)
+        target = slot(block, half)
+        return pltpu.make_async_remote_copy(
+            src_ref=mem_ref.at[pl.ds(start, length)] if block == 0 else target,
+            dst_ref=target,
+            send_sem=send_sems.at[number],
+            recv_sem=recv_sems.at[2 * (block ^ partner) + (half or 0)],
+            device_id=(flipped(me, partner),), device_id_type=MESH,
+        )
+
+    def arrived(block, half):
+        target = slot(block, half)
+        pltpu.make_async_remote_copy(
+            src_ref=target, dst_ref=target, send_sem=send_sems.at[0],
+            recv_sem=recv_sems.at[2 * block + (half or 0)],
+            device_id=(flipped(me, CORE),), device_id_type=MESH,
+        ).wait_recv()
+
+    kept = pltpu.make_async_copy(mem_ref, slot(0, None), local_sem)
+    kept.start()
+    started = []
+    for block, half, group in sends():
+        if block:
+            arrived(block, half)
+        for b, h, partner in group:
+            started.append(copy(b, h, partner, len(started)))
+            started[-1].start()
+        if block == 0:
+            for halo in halos:
+                halo.start()
+    for block, half, group in sends():
+        arrived(block ^ CORE, half)
+    for one in started:
+        one.wait_send()
+    kept.wait()
+    for halo in halos:
+        halo.wait()
+
+
+def exchange(memory, own, size, gather):
+    count = sum(len(group) for _, _, group in sends())
+    whole = memory.shape[0] * (size if gather else 1)
+    anywhere = pl.BlockSpec(memory_space=pl.ANY)
+    return pl.pallas_call(
+        functools.partial(exchange_kernel, size=size, gather=gather),
+        in_specs=[anywhere] * 2,
+        out_specs=[anywhere] * 3,
+        out_shape=[
+            jax.ShapeDtypeStruct((whole,) + memory.shape[1:], memory.dtype),
+            jax.ShapeDtypeStruct((HALO, 2 * D), own.dtype),
+            jax.ShapeDtypeStruct((HALO, 2 * D), own.dtype),
+        ],
+        scratch_shapes=[
+            pltpu.SemaphoreType.DMA,
+            pltpu.SemaphoreType.DMA((count,)),
+            pltpu.SemaphoreType.DMA((64,)),
+            pltpu.SemaphoreType.DMA((4,)),
+        ],
+        compiler_params=pltpu.CompilerParams(collective_id=0, has_side_effects=True),
+        name="exchange",
+    )(memory, own)
+
+
 def attention_kernel(
     slot_ref, edge_ref, q_ref, do_ref, left_ref, own_ref, right_ref, table_ref,
-    att_ref, dq_ref, dkv_ref,
+    att_ref, dq_ref, dleft_ref, dkv_ref, dright_ref,
     kv, acc, sems, *, pairs,
 ):
     step = pl.program_id(0)
@@ -134,8 +268,21 @@
             dq_ref[:, cols(h)] = ((dq_win[h] + unstack(dq_mem, h)) * SCALE).astype(jnp.bfloat16)
 
     done = pl.ds(pl.multiple_of(step * PAIR, PAIR), PAIR)
-    dkv_ref[:, :D] = (acc[done, :D] * SCALE).astype(jnp.bfloat16)
-    dkv_ref[:, D:] = acc[done, D:].astype(jnp.bfloat16)
+    finished = jnp.concatenate(
+        [(acc[done, :D] * SCALE).astype(jnp.bfloat16), acc[done, D:].astype(jnp.bfloat16)], axis=1
+    )
+
+    @pl.when(step == 0)
+    def _():
+        dleft_ref[...] = finished
+
+    @pl.when(jnp.logical_and(step > 0, step <= pairs))
+    def _():
+        dkv_ref[...] = finished
+
+    @pl.when(step == pairs + 1)
+    def _():
+        dright_ref[...] = finished
 
 
 def attention(slots, edges, queries, grad_out, left, own, right, table):
@@ -158,7 +305,9 @@
         out_specs=[
             by_pair,
             by_pair,
-            pl.BlockSpec((PAIR, 2 * D), lambda i, *_: (i, 0)),
+            pl.BlockSpec((HALO, 2 * D), lambda i, *_: (0, 0)),
+            pl.BlockSpec((PAIR, 2 * D), lambda i, *_: (jnp.clip(i - 1, 0, pairs - 1), 0)),
+            pl.BlockSpec((HALO, 2 * D), lambda i, *_: (0, 0)),
         ],
         scratch_shapes=[
             pltpu.VMEM((ext, 2 * D), jnp.bfloat16),
@@ -172,7 +321,9 @@
         out_shape=[
             jax.ShapeDtypeStruct((rows, D), jnp.bfloat16),
             jax.ShapeDtypeStruct((rows, D), jnp.bfloat16),
-            jax.ShapeDtypeStruct((ext, 2 * D), jnp.bfloat16),
+            jax.ShapeDtypeStruct((HALO, 2 * D), jnp.bfloat16),
+            jax.ShapeDtypeStruct((rows, 2 * D), jnp.bfloat16),
+            jax.ShapeDtypeStruct((HALO, 2 * D), jnp.bfloat16),
         ],
         compiler_params=pltpu.CompilerParams(vmem_limit_bytes=56 * 2**20),
         name="attention",
@@ -185,27 +336,25 @@
     me = lax.axis_index("seq")
     up = [(i, i + 1) for i in range(size - 1)]
     down = [(j, i) for i, j in up]
-    left = lax.ppermute(keys_values[rows - HALO :].reshape(HALO, 2 * D), "seq", up)
-    right = lax.ppermute(keys_values[:HALO].reshape(HALO, 2 * D), "seq", down)
-    table = lax.all_gather(memory, "seq", axis=0, tiled=True)
+    own = keys_values.reshape(rows, 2 * D)
+    gather = size == 32
+    table, left, right = exchange(memory, own, size, gather)
+    if not gather:
+        table = lax.all_gather(memory, "seq", axis=0, tiled=True)
     slots = region_slot[block_regions.reshape(-1)]
     edges = jnp.stack([me == 0, me == size - 1]).astype(jnp.int32)
-    own = keys_values.reshape(rows, 2 * D)
-    attended, grad_queries, grads = attention(
+    attended, grad_queries, to_left, grads, to_right = attention(
         slots, edges, queries, grad_out, left, own, right, table
     )
-    from_right = lax.ppermute(grads[:HALO], "seq", down)
-    from_left = lax.ppermute(grads[HALO + rows :], "seq", up)
-    kept = grads[HALO : HALO + rows].astype(jnp.float32)
-    kept = jnp.concatenate(
-        [
-            kept[:HALO] + from_left.astype(jnp.float32),
-            kept[HALO : rows - HALO],
-            kept[rows - HALO :] + from_right.astype(jnp.float32),
-        ],
-        axis=0,
-    )
-    return attended, grad_queries, kept.astype(jnp.bfloat16).reshape(rows, 2, D)
+    from_right = lax.ppermute(to_left, "seq", down)
+    from_left = lax.ppermute(to_right, "seq", up)
+    kept = lax.optimization_barrier(grads.reshape(rows, 2, D))
+    for start, arrived in ((0, from_left), (rows - HALO, from_right)):
+        total = kept[start : start + HALO].astype(jnp.float32) + arrived.reshape(
+            HALO, 2, D
+        ).astype(jnp.float32)
+        kept = lax.dynamic_update_slice(kept, total.astype(jnp.bfloat16), (start, 0, 0))
+    return attended, grad_queries, kept
 
 
 def solution(mesh):

time: 160 us -> 112 us (0.70)
  waiting for transfers between devices: 56.8 us -> 1.81 us
  Pallas kernels: 40.5 us -> 81.2 us
  between operations: 14.2 us -> 0.72 us
  other arithmetic: 14.2 us -> 5.43 us
  starting transfers between devices: 11.6 us -> 4.35 us
  local copies, waits for them, and re-layouts: 22.1 us -> 17.6 us
    all_gather x1 -> x0, waiting for transfers between devices: 46.7 us -> none  [per_device(): table = lax.all_gather(memory, 'seq', axis=0, tiled=True)]
    pallas_call x0 -> x1, Pallas kernels: none -> 39.6 us  [exchange(): pl.pallas_call(functools.partial(exchange_kernel, size=size, gather=gathe...]
    concatenate x3 -> x0, local copies, waits for them, and re-layouts: 8.4 us -> none  [per_device(): jnp.concatenate([kept[:HALO] + from_left.astype(jnp.float32), kept[HALO:r...]
    concatenate x1 -> x0, other arithmetic: 7.79 us -> none  [per_device(): jnp.concatenate([kept[:HALO] + from_left.astype(jnp.float32), kept[HALO:r...]
    reshape x0 -> x1, local copies, waits for them, and re-layouts: none -> 7.79 us  [per_device(): kept = lax.optimization_barrier(grads.reshape(rows, 2, D))]
    ppermute x4 -> x2, waiting for transfers between devices: 9.39 us -> 1.81 us  [the longest x1 1.81 us: per_device(): from_left = lax.ppermute(to_right, 'seq', up)]
    ppermute x4 -> x2, starting transfers between devices: 11.6 us -> 4.35 us  [the longest x1 2.43 us: per_device(): from_right = lax.ppermute(to_left, 'seq', down)]
    slice x3 -> x0, local copies, waits for them, and re-layouts: 6.35 us -> none  [the longest x1 2.32 us: per_device(): from_left = lax.ppermute(grads[HALO + rows:], 'seq', up)]
  transfers between devices with their start and end apart: 5 -> 2, of which waited for: 3 -> 1; matrix products, arithmetic and copies ran while one was open for 11% -> 10% of each run, Pallas kernels for 0% -> 0%
where the time goes in v2:
time: 112 us; the launch traced here: 111 us
  Pallas kernels  81.2 us (72%)
  local copies, waits for them, and re-layouts  17.6 us (16%)
  other arithmetic  5.43 us (5%)
  starting transfers between devices  4.35 us (4%)
  waiting for transfers between devices  1.81 us (2%)
    pallas_call x1, Pallas kernels, attention(): pl.pallas_call(functools.partial(attention_kernel, pairs=pairs), grid_spe...  41.6 us
    pallas_call x1, Pallas kernels, exchange(): pl.pallas_call(functools.partial(exchange_kernel, size=size, gather=gathe...  39.6 us
    reshape x1, local copies, waits for them, and re-layouts, per_device(): kept = lax.optimization_barrier(grads.reshape(rows, 2, D))  7.79 us
    unnamed x4, local copies, waits for them, and re-layouts  6.4 us
    dynamic_update_slice x2, other arithmetic, per_device(): lax.dynamic_update_slice(kept, total.astype(jnp.bfloat16), (start, 0, 0))  4.83 us
    ppermute x1, starting transfers between devices, per_device(): from_right = lax.ppermute(to_left, 'seq', down)  2.43 us
  transfers between devices with their start and end apart: 2, of which 1 were waited for; matrix products, arithmetic and copies ran while one was open for 10% of the time, Pallas kernels for 0%

profile of v2, /device:TPU:1, one launch (start us, length us, event | category | flops | bytes accessed | tf_op | source)
XLA Modules:
  0.0 111.1 jit_solution(1824417541379665855)
XLA Ops:
  0.6 0.0 copy-start
  0.7 0.8 copy.10
  1.4 0.1 reshape.49
  1.5 5.6 %copy.11 = bf16[128,8,2,1024]{3,1,2,0:T(8,128)(2,1)} copy(bf16[128,8,2,1024]{3,2,1,0:T(2,128)(2,1)} %bitcast.8) | data formatting | bytes 8388608
  7.2 0.6 add_convert_fusion.2.edge_ref
  7.8 0.0 copy-done
  7.8 1.3 %gather_fusion = s32[64]{0:T(128)} fusion(s32[128]{0:T(128)S(1)} %copy-done, s32[1024]{0:T(1024)S(1)} %pad_clamp_fusion), kind=kCustom, calls=%fused_computation | custom fusion | bytes 768 | tf_op jit(solution)/shard_map/gather | solution.py:344
  9.0 39.6 %exchange.1 = (bf16[128,64,256]{2,1,0:T(8,128)(2,1)}, bf16[128,2048]{1,0:T(8,128)(2,1)}, bf16[128,2048]{1,0:T(8,128)(2,1)}) custom-call(bf16[4,64,256]{2,1,0:T(8,128)(2,1)} %mem_ref.1, bf16[1024,2048]{1,0:T(8,128)(2,1)} %bitcast.6), custom_call_target="tpu_custom_call" | custom-call | tf_op jit(solution)/shard_map/exchange/pallas_call | solution.py:147
  48.7 41.6 %attention.1 = (bf16[1024,1024]{1,0:T(8,128)(2,1)}, bf16[1024,1024]{1,0:T(8,128)(2,1)}, bf16[128,2048]{1,0:T(8,128)(2,1)}, bf16[1024,2048]{1,0:T(8,128)(2,1)}, bf16[128,2048]{1,0:T(8,128)(2,1)}) custom-call(s32[64]{0:T(128)} %gather_fusion, s32[2]{0:T(128)} %add_convert_fusion.2.edge_ref, bf16[1024,1024]{1,0:T(8,128)(2,1)} %q_ref.1, ...), custom_call_target="tpu_custom_call" | custom-call | tf_op jit(solution)/shard_map/attention/pallas_call | solution.py:318
  90.3 1.9 %collective-permute-start = (bf16[128,2048]{1,0:T(8,128)(2,1)}, bf16[128,2048]{1,0:T(8,128)(2,1)S(1)}, u32[]{:S(2)}, u32[]{:S(2)}) collective-permute-start(bf16[128,2048]{1,0:T(8,128)(2,1)} %get-tuple-element.17), channel_id=1, source_target_pairs={{0,1},{1,2},{2,3},{3,4},{4,5},{5,6},{6,7},{7,8},{8,9},{9,10},{10,1... | collective-permute-start | bytes 1572872 | tf_op jit(solution)/shard_map/ppermute | solution.py:350
  92.2 2.4 %collective-permute-start.1 = (bf16[128,2048]{1,0:T(8,128)(2,1)}, bf16[128,2048]{1,0:T(8,128)(2,1)S(1)}, u32[]{:S(2)}, u32[]{:S(2)}) collective-permute-start(bf16[128,2048]{1,0:T(8,128)(2,1)} %get-tuple-element.18), channel_id=1, source_target_pairs={{1,0},{2,1},{3,2},{4,3},{5,4},{6,5},{7,6},{8,7},{9,8},{10,9},{11,1... | collective-permute-start | bytes 1572872 | tf_op jit(solution)/shard_map/ppermute | solution.py:349
  94.6 7.8 %reshape.51 = bf16[1024,2,1024]{2,1,0:T(2,128)(2,1)} reshape(bf16[1024,2048]{1,0:T(8,128)(2,1)} %get-tuple-element.16) | data formatting | bytes 8388608 | tf_op jit(solution)/shard_map/reshape | solution.py:351
  102.4 1.8 %collective-permute-done = bf16[128,2048]{1,0:T(8,128)(2,1)S(1)} collective-permute-done((bf16[128,2048]{1,0:T(8,128)(2,1)}, bf16[128,2048]{1,0:T(8,128)(2,1)S(1)}, u32[]{:S(2)}, u32[]{:S(2)}) %collective-permute-start) | collective-permute-done | bytes 524320 | tf_op jit(solution)/shard_map/ppermute | solution.py:350
  104.2 1.0 reshape.52
  105.3 2.4 %fusion = bf16[1024,2,1024]{2,1,0:T(2,128)(2,1)} fusion(bf16[1024,2,1024]{2,1,0:T(2,128)(2,1)} %reshape.51, f32[128,2,1024]{2,1,0:T(2,128)S(1)} %reshape.52), kind=kLoop, calls=%fused_computation.3 | loop fusion | flops 786432 | bytes 2097152 | tf_op jit(solution)/shard_map/dynamic_update_slice | solution.py:356
  107.7 0.0 collective-permute-done.1
  107.7 1.0 reshape.53
  108.7 2.4 %fusion.1 = bf16[1024,2,1024]{2,1,0:T(2,128)(2,1)} fusion(bf16[1024,2,1024]{2,1,0:T(2,128)(2,1)} %fusion, f32[128,2,1024]{2,1,0:T(2,128)S(1)} %reshape.53), kind=kLoop, calls=%fused_computation.4 | loop fusion | flops 786432 | bytes 2097152 | tf_op jit(solution)/shard_map/dynamic_update_slice | solution.py:356
  (2 shorter events, 0.0 us)
Async XLA Ops:
  0.6 7.1 %copy-start = (s32[128]{0:T(128)S(1)}, s32[128]{0:T(128)}, u32[]{:S(2)}) copy-start(s32[128]{0:T(128)} %param.10) | copy-start | bytes 1540
  90.3 14.0 %collective-permute-start = (bf16[128,2048]{1,0:T(8,128)(2,1)}, bf16[128,2048]{1,0:T(8,128)(2,1)S(1)}, u32[]{:S(2)}, u32[]{:S(2)}) collective-permute-start(bf16[128,2048]{1,0:T(8,128)(2,1)} %get-tuple-element.17), channel_id=1, source_target_pairs={{0,1},{1,2},{2,3},{3,4},{4,5},{5,6},{6,7},{7,8},{8,9},{9,10},{10,1... | collective-permute-start | bytes 1572872 | tf_op jit(solution)/shard_map/ppermute | solution.py:350
  92.2 15.5 %collective-permute-start.1 = (bf16[128,2048]{1,0:T(8,128)(2,1)}, bf16[128,2048]{1,0:T(8,128)(2,1)S(1)}, u32[]{:S(2)}, u32[]{:S(2)}) collective-permute-start(bf16[128,2048]{1,0:T(8,128)(2,1)} %get-tuple-element.18), channel_id=1, source_target_pairs={{1,0},{2,1},{3,2},{4,3},{5,4},{6,5},{7,6},{8,7},{9,8},{10,9},{11,1... | collective-permute-start | bytes 1572872 | tf_op jit(solution)/shard_map/ppermute | solution.py:349

commit v3 on v2

--- a/solution.py
+++ b/solution.py
@@ -64,7 +64,12 @@
     return groups
 
 
-def exchange_kernel(mem_ref, own_ref, table_ref, left_ref, right_ref, local_sem, send_sems, recv_sems, halo_sems, *, size, gather):
+def exchange_kernel(
+    mem_ref, own_ref, q_ref, do_ref,
+    table_ref, left_ref, right_ref, e_ref, dp_ref, out_ref, stat_ref,
+    kv, q, do, e_own, dp_own, out_own, stat_own,
+    local_sem, send_sems, recv_sems, halo_sems, load_sems, store_sems, *, size, gather,
+):
     me = lax.axis_index("seq")
     after, before = lax.rem(me + 1, size), lax.rem(me + size - 1, size)
     masks = (CORE, X, Y, Z, ZZ) if gather else ()
@@ -85,12 +90,6 @@
             ((rows - HALO, left_ref, after), (0, right_ref, before))
         )
     ]
-    if not gather:
-        for halo in halos:
-            halo.start()
-        for halo in halos:
-            halo.wait()
-        return
     blocks = mem_ref.shape[0]
 
     def part(half):
@@ -119,65 +118,161 @@
             device_id=(flipped(me, CORE),), device_id_type=MESH,
         ).wait_recv()
 
-    kept = pltpu.make_async_copy(mem_ref, slot(0, None), local_sem)
-    kept.start()
+    groups = sends() if gather else []
     started = []
-    for block, half, group in sends():
-        if block:
-            arrived(block, half)
-        for b, h, partner in group:
-            started.append(copy(b, h, partner, len(started)))
-            started[-1].start()
-        if block == 0:
-            for halo in halos:
-                halo.start()
-    for block, half, group in sends():
+
+    def forward(first, last):
+        for block, half, group in groups[first:last]:
+            if block:
+                arrived(block, half)
+            for b, h, partner in group:
+                started.append(copy(b, h, partner, len(started)))
+                started[-1].start()
+
+    pairs = rows // PAIR
+    row = lax.broadcasted_iota(jnp.int32, (PAIR, PAIR), 0)
+    lane = lax.broadcasted_iota(jnp.int32, (PAIR, PAIR), 1)
+    stores = []
+
+    def window_part(p):
+        see_left = jnp.logical_or(row < BLK, lane >= BLK)
+        see_right = jnp.logical_or(row >= BLK, lane < BLK)
+        if p == 0:
+            see_left = jnp.logical_and(see_left, me > 0)
+        if p == pairs - 1:
+            see_right = jnp.logical_and(see_right, me < size - 1)
+        bias_left = jnp.where(see_left, 0.0, NEG_FILL)
+        bias_right = jnp.where(see_right, 0.0, NEG_FILL)
+        mine = pl.ds(p * PAIR, PAIR)
+        window = pl.ds(p * PAIR, SPAN)
+
+        def head(h, carry):
+            columns = pl.ds(pl.multiple_of(h * DH, DH), DH)
+            wide = pl.ds(pl.multiple_of(h * SPAN, DH), SPAN)
+            values = kv[window, pl.ds(pl.multiple_of(D + h * DH, DH), DH)]
+            sw = dot(q[mine, columns], kv[window, columns], NT)
+            dp_own[mine, wide] = dot(do[mine, columns], values, NT)
+            sw = jnp.concatenate(
+                [sw[:, :PAIR] + bias_left, sw[:, PAIR : 2 * PAIR], sw[:, 2 * PAIR :] + bias_right],
+                axis=1,
+            )
+            top = jnp.max(sw, axis=1, keepdims=True)
+            ew = jnp.exp2((sw - top) * EXP2_SCALE)
+            e_own[mine, wide] = ew
+            total = jnp.sum(ew, axis=1, keepdims=True)
+            stat_own[mine, columns] = jnp.where(lane < BLK, top, total)
+            out_own[mine, columns] = dot(ew.astype(jnp.bfloat16), values, NN)
+            return carry
+
+        lax.fori_loop(0, H, head, 0, unroll=2)
+        for src, dst in ((e_own, e_ref), (dp_own, dp_ref), (out_own, out_ref), (stat_own, stat_ref)):
+            stores.append(
+                pltpu.make_async_copy(src.at[mine], dst.at[mine], store_sems.at[len(stores)])
+            )
+            stores[-1].start()
+
+    forward(0, 1)
+    for halo in halos:
+        halo.start()
+    loads = [
+        pltpu.make_async_copy(src, dst, load_sems.at[i])
+        for i, (src, dst) in enumerate((
+            (own_ref, kv.at[pl.ds(HALO, rows)]), (q_ref, q), (do_ref, do),
+            (left_ref, kv.at[pl.ds(0, HALO)]), (right_ref, kv.at[pl.ds(HALO + rows, HALO)]),
+        ))
+    ]
+    for load in loads[:3]:
+        load.start()
+    if gather:
+        kept = pltpu.make_async_copy(mem_ref, slot(0, None), local_sem)
+        kept.start()
+    for load in loads[:3]:
+        load.wait()
+    window_part(1)
+    forward(1, 3)
+    window_part(2)
+    forward(3, 6)
+    window_part(3)
+    forward(6, 8)
+    for p in range(4, pairs - 2):
+        window_part(p)
+    forward(8, 10)
+    for halo in halos:
+        halo.wait()
+    for load in loads[3:]:
+        load.start()
+    window_part(pairs - 2)
+    for load in loads[3:]:
+        load.wait()
+    forward(10, 12)
+    window_part(0)
+    forward(12, 14)
+    window_part(pairs - 1)
+    forward(14, len(groups))
+    for block, half, group in groups:
         arrived(block ^ CORE, half)
     for one in started:
         one.wait_send()
-    kept.wait()
-    for halo in halos:
-        halo.wait()
-
-
-def exchange(memory, own, size, gather):
+    if gather:
+        kept.wait()
+    for store in stores:
+        store.wait()
+
+
+def exchange(memory, own, queries, grad_out, size, gather):
     count = sum(len(group) for _, _, group in sends())
+    rows = own.shape[0]
     whole = memory.shape[0] * (size if gather else 1)
     anywhere = pl.BlockSpec(memory_space=pl.ANY)
+    made = [
+        (rows, H * SPAN),
+        (rows, H * SPAN),
+        (rows, D),
+        (rows, D),
+    ]
     return pl.pallas_call(
         functools.partial(exchange_kernel, size=size, gather=gather),
-        in_specs=[anywhere] * 2,
-        out_specs=[anywhere] * 3,
+        in_specs=[anywhere] * 4,
+        out_specs=[anywhere] * 7,
         out_shape=[
             jax.ShapeDtypeStruct((whole,) + memory.shape[1:], memory.dtype),
             jax.ShapeDtypeStruct((HALO, 2 * D), own.dtype),
             jax.ShapeDtypeStruct((HALO, 2 * D), own.dtype),
-        ],
+        ] + [jax.ShapeDtypeStruct(shape, jnp.float32) for shape in made],
         scratch_shapes=[
+            pltpu.VMEM((rows + 2 * HALO, 2 * D), jnp.bfloat16),
+            pltpu.VMEM((rows, D), jnp.bfloat16),
+            pltpu.VMEM((rows, D), jnp.bfloat16),
+        ] + [pltpu.VMEM(shape, jnp.float32) for shape in made] + [
             pltpu.SemaphoreType.DMA,
             pltpu.SemaphoreType.DMA((count,)),
             pltpu.SemaphoreType.DMA((64,)),
             pltpu.SemaphoreType.DMA((4,)),
+            pltpu.SemaphoreType.DMA((5,)),
+            pltpu.SemaphoreType.DMA((4 * rows // PAIR,)),
         ],
-        compiler_params=pltpu.CompilerParams(collective_id=0, has_side_effects=True),
+        compiler_params=pltpu.CompilerParams(
+            collective_id=0, has_side_effects=True, vmem_limit_bytes=56 * 2**20
+        ),
         name="exchange",
-    )(memory, own)
+    )(memory, own, queries, grad_out)
 
 
 def attention_kernel(
-    slot_ref, edge_ref, q_ref, do_ref, left_ref, own_ref, right_ref, table_ref,
+    slot_ref, q_ref, do_ref, e_ref, dp_ref, out_ref, stat_ref, left_ref, own_ref, right_ref, table_ref,
     att_ref, dq_ref, dleft_ref, dkv_ref, dright_ref,
-    kv, acc, sems, *, pairs,
+    keys, acc, sems, *, pairs,
 ):
     step = pl.program_id(0)
 
     @pl.when(step == 0)
     def _():
         rows = own_ref.shape[0]
+        half = pl.ds(0, D)
         copies = [
-            pltpu.make_async_copy(left_ref, kv.at[pl.ds(0, HALO)], sems.at[0]),
-            pltpu.make_async_copy(own_ref, kv.at[pl.ds(HALO, rows)], sems.at[1]),
-            pltpu.make_async_copy(right_ref, kv.at[pl.ds(HALO + rows, HALO)], sems.at[2]),
+            pltpu.make_async_copy(left_ref.at[:, half], keys.at[pl.ds(0, HALO)], sems.at[0]),
+            pltpu.make_async_copy(own_ref.at[:, half], keys.at[pl.ds(HALO, rows)], sems.at[1]),
+            pltpu.make_async_copy(right_ref.at[:, half], keys.at[pl.ds(HALO + rows, HALO)], sems.at[2]),
         ]
         for copy in copies:
             copy.start()
@@ -189,18 +284,6 @@
     def _():
         base = pl.multiple_of(step * PAIR, PAIR)
         window = pl.ds(base, SPAN)
-        row = lax.broadcasted_iota(jnp.int32, (PAIR, PAIR), 0)
-        lane = lax.broadcasted_iota(jnp.int32, (PAIR, PAIR), 1)
-        no_left = jnp.logical_and(step == 0, edge_ref[0] == 1)
-        no_right = jnp.logical_and(step == pairs - 1, edge_ref[1] == 1)
-        bias_left = jnp.where(
-            jnp.logical_and(jnp.logical_or(row < BLK, lane >= BLK), jnp.logical_not(no_left)),
-            0.0, NEG_FILL,
-        )
-        bias_right = jnp.where(
-            jnp.logical_and(jnp.logical_or(row >= BLK, lane < BLK), jnp.logical_not(no_right)),
-            0.0, NEG_FILL,
-        )
 
         mem_keys, mem_values = [], []
         for b in range(2):
@@ -223,43 +306,44 @@
 
         q = [q_ref[:, cols(h)] for h in range(H)]
         mem_scores = [dot(x, k, NT) for x, k in zip(stack(q), mem_keys)]
-        e_win, e_mem, p_win, p_mem, totals, out_win = [], [], [], [], [], []
+        e_mem, inverses, shares = [], [], []
         for h in range(H):
-            sw = dot(q[h], kv[window, cols(h)], NT)
-            sw = jnp.concatenate(
-                [sw[:, :PAIR] + bias_left, sw[:, PAIR : 2 * PAIR], sw[:, 2 * PAIR :] + bias_right],
-                axis=1,
-            )
             sm = unstack(mem_scores, h)
-            top = jnp.maximum(
-                jnp.max(sw, axis=1, keepdims=True), jnp.max(sm, axis=1, keepdims=True)
-            )
-            ew = jnp.exp2((sw - top) * EXP2_SCALE)
+            win_top = stat_ref[:, h * DH : h * DH + 1]
+            win_total = stat_ref[:, h * DH + BLK : h * DH + BLK + 1]
+            top = jnp.maximum(win_top, jnp.max(sm, axis=1, keepdims=True))
             em = jnp.exp2((sm - top) * EXP2_SCALE)
-            totals.append(jnp.sum(ew, axis=1, keepdims=True) + jnp.sum(em, axis=1, keepdims=True))
-            e_win.append(ew)
+            share = jnp.exp2((win_top - top) * EXP2_SCALE)
+            inverse = 1.0 / (share * win_total + jnp.sum(em, axis=1, keepdims=True))
             e_mem.append(em)
-            p_win.append(ew.astype(jnp.bfloat16))
-            p_mem.append(em.astype(jnp.bfloat16))
-            out_win.append(dot(p_win[h], kv[window, slice(D + h * DH, D + (h + 1) * DH)], NN))
-        out_mem = [dot(x, v, NN) for x, v in zip(stack(p_mem), mem_values)]
-        scaled, deltas = [], []
+            inverses.append(inverse)
+            shares.append(share * inverse)
+        out_mem = [
+            dot(x, v, NN)
+            for x, v in zip(stack([em.astype(jnp.bfloat16) for em in e_mem]), mem_values)
+        ]
+        low_win, low_mem, deltas, mem_deltas = [], [], [], []
         for h in range(H):
-            inverse = 1.0 / totals[h]
-            out = (out_win[h] + unstack(out_mem, h)) * inverse
+            out = out_ref[:, cols(h)] * shares[h] + unstack(out_mem, h) * inverses[h]
             att_ref[:, cols(h)] = out.astype(jnp.bfloat16)
-            low = (do_ref[:, cols(h)].astype(jnp.float32) * inverse).astype(jnp.bfloat16)
-            scaled.append(low)
-            deltas.append(jnp.sum(low.astype(jnp.float32) * out, axis=1, keepdims=True))
-        mem_probs = [dot(x, v, NT) for x, v in zip(stack(scaled), mem_values)]
+            grad = do_ref[:, cols(h)].astype(jnp.float32)
+            low_win.append((grad * shares[h]).astype(jnp.bfloat16))
+            low_mem.append((grad * inverses[h]).astype(jnp.bfloat16))
+            deltas.append(jnp.sum(grad * out, axis=1, keepdims=True))
+            mem_deltas.append(jnp.sum(low_mem[h].astype(jnp.float32) * out, axis=1, keepdims=True))
+        mem_probs = [dot(x, v, NT) for x, v in zip(stack(low_mem), mem_values)]
         ds_mem, dq_win = [], []
         for h in range(H):
+            wide = slice(h * SPAN, (h + 1) * SPAN)
+            ew = e_ref[:, wide]
+            dsw = ((ew * shares[h]) * (dp_ref[:, wide] - deltas[h])).astype(jnp.bfloat16)
+            ds_mem.append((e_mem[h] * (unstack(mem_probs, h) - mem_deltas[h])).astype(jnp.bfloat16))
+            dq_win.append(dot(dsw, keys[window, cols(h)], NN))
             vcols = slice(D + h * DH, D + (h + 1) * DH)
-            pw = dot(scaled[h], kv[window, vcols], NT)
-            dsw = (e_win[h] * (pw - deltas[h])).astype(jnp.bfloat16)
-            ds_mem.append((e_mem[h] * (unstack(mem_probs, h) - deltas[h])).astype(jnp.bfloat16))
-            dq_win.append(dot(dsw, kv[window, cols(h)], NN))
-            for columns, low, rows in ((cols(h), dsw, q[h]), (vcols, p_win[h], scaled[h])):
+            for columns, low, rows in (
+                (cols(h), dsw, q[h]),
+                (vcols, ew.astype(jnp.bfloat16), low_win[h]),
+            ):
                 term = dot(low, rows, TN)
                 acc[pl.ds(base, SPAN - PAIR), columns] += term[: SPAN - PAIR]
                 acc[pl.ds(base + SPAN - PAIR, PAIR), columns] = term[SPAN - PAIR :]
@@ -285,16 +369,21 @@
         dright_ref[...] = finished
 
 
-def attention(slots, edges, queries, grad_out, left, own, right, table):
+def attention(slots, queries, grad_out, e, dp, out, stat, left, own, right, table):
     rows = queries.shape[0]
     pairs = rows // PAIR
     steps = pairs + 2 * HALO // PAIR
     ext = rows + 2 * HALO
     by_pair = pl.BlockSpec((PAIR, D), lambda i, *_: (jnp.minimum(i, pairs - 1), 0))
+    wide = pl.BlockSpec((PAIR, H * SPAN), lambda i, *_: (jnp.minimum(i, pairs - 1), 0))
     spec = pltpu.PrefetchScalarGridSpec(
-        num_scalar_prefetch=2,
+        num_scalar_prefetch=1,
         grid=(steps,),
         in_specs=[
+            by_pair,
+            by_pair,
+            wide,
+            wide,
             by_pair,
             by_pair,
             pl.BlockSpec(memory_space=pl.ANY),
@@ -310,7 +399,7 @@
             pl.BlockSpec((HALO, 2 * D), lambda i, *_: (0, 0)),
         ],
         scratch_shapes=[
-            pltpu.VMEM((ext, 2 * D), jnp.bfloat16),
+            pltpu.VMEM((ext, D), jnp.bfloat16),
             pltpu.VMEM((ext, 2 * D), jnp.float32),
             pltpu.SemaphoreType.DMA((3,)),
         ],
@@ -327,24 +416,24 @@
         ],
         compiler_params=pltpu.CompilerParams(vmem_limit_bytes=56 * 2**20),
         name="attention",
-    )(slots, edges, queries, grad_out, left, own, right, table)
+    )(slots, queries, grad_out, e, dp, out, stat, left, own, right, table)
 
 
 def per_device(queries, keys_values, memory, block_regions, region_slot, grad_out):
     rows = queries.shape[0]
     size = lax.axis_size("seq")
-    me = lax.axis_index("seq")
     up = [(i, i + 1) for i in range(size - 1)]
     down = [(j, i) for i, j in up]
     own = keys_values.reshape(rows, 2 * D)
     gather = size == 32
-    table, left, right = exchange(memory, own, size, gather)
+    table, left, right, e, dp, out, stat = exchange(
+        memory, own, queries, grad_out, size, gather
+    )
     if not gather:
         table = lax.all_gather(memory, "seq", axis=0, tiled=True)
     slots = region_slot[block_regions.reshape(-1)]
-    edges = jnp.stack([me == 0, me == size - 1]).astype(jnp.int32)
     attended, grad_queries, to_left, grads, to_right = attention(
-        slots, edges, queries, grad_out, left, own, right, table
+        slots, queries, grad_out, e, dp, out, stat, left, own, right, table
     )
     from_right = lax.ppermute(to_left, "seq", down)
     from_left = lax.ppermute(to_right, "seq", up)

time: 112 us -> 119 us (1.062)
  Pallas kernels: 81.2 us -> 86.3 us
  starting transfers between devices: 4.35 us -> 5.74 us
    pallas_call x1, Pallas kernels: 41.6 us -> 44.4 us  [attention(): pl.pallas_call(functools.partial(attention_kernel, pairs=pairs), grid_spe...]
    pallas_call x1, Pallas kernels: 39.6 us -> 41.9 us  [exchange(): pl.pallas_call(functools.partial(exchange_kernel, size=size, gather=gathe...]
    ppermute x1, starting transfers between devices: 1.92 us -> 3.64 us  [per_device(): from_left = lax.ppermute(to_right, 'seq', up)]
    unnamed x4 -> x6, local copies, waits for them, and re-layouts: 6.4 us -> 6.42 us
where the time goes in v3:
time: 119 us; the launch traced here: 117 us
  Pallas kernels  86.3 us (73%)
  local copies, waits for them, and re-layouts  17.7 us (15%)
  starting transfers between devices  5.74 us (5%)
  other arithmetic  4.84 us (4%)
  waiting for transfers between devices  2.13 us (2%)
    pallas_call x1, Pallas kernels, attention(): pl.pallas_call(functools.partial(attention_kernel, pairs=pairs), grid_spe...  44.4 us
    pallas_call x1, Pallas kernels, exchange(): pl.pallas_call(functools.partial(exchange_kernel, size=size, gather=gathe...  41.9 us
    reshape x1, local copies, waits for them, and re-layouts, per_device(): kept = lax.optimization_barrier(grads.reshape(rows, 2, D))  7.79 us
    unnamed x6, local copies, waits for them, and re-layouts  6.42 us
    dynamic_update_slice x2, other arithmetic, per_device(): lax.dynamic_update_slice(kept, total.astype(jnp.bfloat16), (start, 0, 0))  4.83 us
    ppermute x1, starting transfers between devices, per_device(): from_left = lax.ppermute(to_right, 'seq', up)  3.64 us
  transfers between devices with their start and end apart: 2, of which 1 were waited for; matrix products, arithmetic and copies ran while one was open for 10% of the time, Pallas kernels for 0%

profile of v3, /device:TPU:1, one launch (start us, length us, event | category | flops | bytes accessed | tf_op | source)
XLA Modules:
  0.0 117.4 jit_solution(15130066939769675504)
XLA Ops:
  0.6 0.0 copy-start
  0.6 0.8 copy.10
  1.4 0.1 reshape.49
  1.5 5.6 %copy.11 = bf16[128,8,2,1024]{3,1,2,0:T(8,128)(2,1)} copy(bf16[128,8,2,1024]{3,2,1,0:T(2,128)(2,1)} %bitcast.6) | data formatting | bytes 8388608
  7.2 0.0 copy-done
  7.2 1.4 %gather_fusion = s32[64]{0:T(128)} fusion(s32[128]{0:T(128)S(1)} %copy-done, s32[1024]{0:T(1024)S(1)} %pad_clamp_fusion), kind=kCustom, calls=%fused_computation | custom fusion | bytes 768 | tf_op jit(solution)/shard_map/gather | solution.py:434
  8.5 41.9 %exchange.1 = (bf16[128,64,256]{2,1,0:T(8,128)(2,1)}, bf16[128,2048]{1,0:T(8,128)(2,1)}, bf16[128,2048]{1,0:T(8,128)(2,1)}, f32[1024,3072]{1,0:T(8,128)}, f32[10...) custom-call(bf16[4,64,256]{2,1,0:T(8,128)(2,1)} %mem_ref.1, bf16[1024,2048]{1,0:T(8,128)(2,1)} %bitcast.4, ...), custom_call_target="tpu_custom_call" | custom-call | tf_op jit(solution)/shard_map/exchange/pallas_call | solution.py:233
  50.4 44.4 %attention.1 = (bf16[1024,1024]{1,0:T(8,128)(2,1)}, bf16[1024,1024]{1,0:T(8,128)(2,1)}, bf16[128,2048]{1,0:T(8,128)(2,1)}, bf16[1024,2048]{1,0:T(8,128)(2,1)}, bf16[128,2048]{1,0:T(8,128)(2,1)}) custom-call(s32[64]{0:T(128)} %gather_fusion, bf16[1024,1024]{1,0:T(8,128)(2,1)} %q_ref.3, bf16[1024,1024]{1,0:T(8,128)(2,1)} %do_ref.3, ...), custom_call_target="tpu_custom_call" | custom-call | tf_op jit(solution)/shard_map/attention/pallas_call | solution.py:407
  94.8 3.6 %collective-permute-start = (bf16[128,2048]{1,0:T(8,128)(2,1)}, bf16[128,2048]{1,0:T(8,128)(2,1)S(1)}, u32[]{:S(2)}, u32[]{:S(2)}) collective-permute-start(bf16[128,2048]{1,0:T(8,128)(2,1)} %get-tuple-element.25), channel_id=1, source_target_pairs={{0,1},{1,2},{2,3},{3,4},{4,5},{5,6},{6,7},{7,8},{8,9},{9,10},{10,1... | collective-permute-start | bytes 1572872 | tf_op jit(solution)/shard_map/ppermute | solution.py:439
  98.5 2.1 %collective-permute-start.1 = (bf16[128,2048]{1,0:T(8,128)(2,1)}, bf16[128,2048]{1,0:T(8,128)(2,1)S(1)}, u32[]{:S(2)}, u32[]{:S(2)}) collective-permute-start(bf16[128,2048]{1,0:T(8,128)(2,1)} %get-tuple-element.26), channel_id=1, source_target_pairs={{1,0},{2,1},{3,2},{4,3},{5,4},{6,5},{7,6},{8,7},{9,8},{10,9},{11,1... | collective-permute-start | bytes 1572872 | tf_op jit(solution)/shard_map/ppermute | solution.py:438
  100.6 0.0 copy-start.1
  100.6 7.8 %reshape.51 = bf16[1024,2,1024]{2,1,0:T(2,128)(2,1)} reshape(bf16[1024,2048]{1,0:T(8,128)(2,1)} %get-tuple-element.24) | data formatting | bytes 8388608 | tf_op jit(solution)/shard_map/reshape | solution.py:440
  108.4 2.1 %collective-permute-done = bf16[128,2048]{1,0:T(8,128)(2,1)S(1)} collective-permute-done((bf16[128,2048]{1,0:T(8,128)(2,1)}, bf16[128,2048]{1,0:T(8,128)(2,1)S(1)}, u32[]{:S(2)}, u32[]{:S(2)}) %collective-permute-start) | collective-permute-done | bytes 524320 | tf_op jit(solution)/shard_map/ppermute | solution.py:439
  110.5 1.0 reshape.52
  111.6 2.4 %fusion = bf16[1024,2,1024]{2,1,0:T(2,128)(2,1)} fusion(bf16[1024,2,1024]{2,1,0:T(2,128)(2,1)} %reshape.51, f32[128,2,1024]{2,1,0:T(2,128)S(1)} %reshape.52), kind=kLoop, calls=%fused_computation.3 | loop fusion | flops 786432 | bytes 2097152 | tf_op jit(solution)/shard_map/dynamic_update_slice | solution.py:445
  114.0 0.0 collective-permute-done.1
  114.0 1.0 reshape.53
  115.0 2.4 %fusion.1 = bf16[1024,2,1024]{2,1,0:T(2,128)(2,1)} fusion(bf16[1024,2,1024]{2,1,0:T(2,128)(2,1)} %fusion, f32[128,2,1024]{2,1,0:T(2,128)S(1)} %reshape.53), kind=kLoop, calls=%fused_computation.4 | loop fusion | flops 786432 | bytes 2097152 | tf_op jit(solution)/shard_map/dynamic_update_slice | solution.py:445
  117.4 0.0 copy-done.1
  (2 shorter events, 0.0 us)
Async XLA Ops:
  0.6 6.5 %copy-start = (s32[128]{0:T(128)S(1)}, s32[128]{0:T(128)}, u32[]{:S(2)}) copy-start(s32[128]{0:T(128)} %param.10) | copy-start | bytes 1540
  94.8 15.7 %collective-permute-start = (bf16[128,2048]{1,0:T(8,128)(2,1)}, bf16[128,2048]{1,0:T(8,128)(2,1)S(1)}, u32[]{:S(2)}, u32[]{:S(2)}) collective-permute-start(bf16[128,2048]{1,0:T(8,128)(2,1)} %get-tuple-element.25), channel_id=1, source_target_pairs={{0,1},{1,2},{2,3},{3,4},{4,5},{5,6},{6,7},{7,8},{8,9},{9,10},{10,1... | collective-permute-start | bytes 1572872 | tf_op jit(solution)/shard_map/ppermute | solution.py:439
  98.5 15.5 %collective-permute-start.1 = (bf16[128,2048]{1,0:T(8,128)(2,1)}, bf16[128,2048]{1,0:T(8,128)(2,1)S(1)}, u32[]{:S(2)}, u32[]{:S(2)}) collective-permute-start(bf16[128,2048]{1,0:T(8,128)(2,1)} %get-tuple-element.26), channel_id=1, source_target_pairs={{1,0},{2,1},{3,2},{4,3},{5,4},{6,5},{7,6},{8,7},{9,8},{10,9},{11,1... | collective-permute-start | bytes 1572872 | tf_op jit(solution)/shard_map/ppermute | solution.py:438
  100.6 16.8 %copy-start.1 = (s32[128]{0:T(128)S(1)}, s32[128]{0:T(128)}, u32[]{:S(2)}) copy-start(s32[128]{0:T(128)} %param.10) | copy-start | bytes 1540

commit v4 on v2

--- a/solution.py
+++ b/solution.py
@@ -30,6 +30,10 @@
 
 def dot(a, b, dims):
     return lax.dot_general(a, b, dims, preferred_element_type=jnp.float32)
+
+
+def across(a, b):
+    return dot(a, b, TN)
 
 
 def flipped(number, mask):
@@ -165,24 +169,42 @@
 
 
 def attention_kernel(
-    slot_ref, edge_ref, q_ref, do_ref, left_ref, own_ref, right_ref, table_ref,
+    regions_ref, slot_ref, me_ref, q_ref, do_ref, left_ref, own_ref, right_ref, far_ref,
     att_ref, dq_ref, dleft_ref, dkv_ref, dright_ref,
-    kv, acc, sems, *, pairs,
+    kv, acc, table_ref, sems, *, pairs, size,
 ):
     step = pl.program_id(0)
 
+    rows, stored = own_ref.shape[0], far_ref.shape[0] // 2
+    near = SPAN - HALO
+    first = [
+        pltpu.make_async_copy(left_ref, kv.at[pl.ds(0, HALO)], sems.at[0]),
+        pltpu.make_async_copy(own_ref.at[pl.ds(0, near)], kv.at[pl.ds(HALO, near)], sems.at[1]),
+        pltpu.make_async_copy(far_ref.at[pl.ds(0, stored)], table_ref.at[pl.ds(0, stored)], sems.at[2]),
+        pltpu.make_async_copy(
+            far_ref.at[pl.ds(stored, stored)], table_ref.at[pl.ds(stored, stored)], sems.at[3]
+        ),
+    ]
+    later = [
+        pltpu.make_async_copy(
+            own_ref.at[pl.ds(near, rows - near)],
+            kv.at[pl.ds(HALO + near, rows - near)],
+            sems.at[4],
+        ),
+        pltpu.make_async_copy(right_ref, kv.at[pl.ds(HALO + rows, HALO)], sems.at[5]),
+    ]
+
     @pl.when(step == 0)
     def _():
-        rows = own_ref.shape[0]
-        copies = [
-            pltpu.make_async_copy(left_ref, kv.at[pl.ds(0, HALO)], sems.at[0]),
-            pltpu.make_async_copy(own_ref, kv.at[pl.ds(HALO, rows)], sems.at[1]),
-            pltpu.make_async_copy(right_ref, kv.at[pl.ds(HALO + rows, HALO)], sems.at[2]),
-        ]
-        for copy in copies:
+        for copy in first + later:
             copy.start()
         acc[pl.ds(0, SPAN - PAIR), :] = jnp.zeros((SPAN - PAIR, 2 * D), jnp.float32)
-        for copy in copies:
+        for copy in first:
+            copy.wait()
+
+    @pl.when(step == 1)
+    def _():
+        for copy in later:
             copy.wait()
 
     @pl.when(step < pairs)
@@ -191,8 +213,8 @@
         window = pl.ds(base, SPAN)
         row = lax.broadcasted_iota(jnp.int32, (PAIR, PAIR), 0)
         lane = lax.broadcasted_iota(jnp.int32, (PAIR, PAIR), 1)
-        no_left = jnp.logical_and(step == 0, edge_ref[0] == 1)
-        no_right = jnp.logical_and(step == pairs - 1, edge_ref[1] == 1)
+        no_left = jnp.logical_and(step == 0, me_ref[0] == 0)
+        no_right = jnp.logical_and(step == pairs - 1, me_ref[0] == size - 1)
         bias_left = jnp.where(
             jnp.logical_and(jnp.logical_or(row < BLK, lane >= BLK), jnp.logical_not(no_left)),
             0.0, NEG_FILL,
@@ -204,7 +226,7 @@
 
         mem_keys, mem_values = [], []
         for b in range(2):
-            parts = [table_ref[slot_ref[(step * 2 + b) * MEM + m]] for m in range(MEM)]
+            parts = [table_ref[slot_ref[regions_ref[step * 2 + b, m]]] for m in range(MEM)]
             rows = jnp.concatenate(parts, axis=0)
             mem_keys.append(rows[:, :DH])
             mem_values.append(rows[:, DH:])
@@ -260,7 +282,7 @@
             ds_mem.append((e_mem[h] * (unstack(mem_probs, h) - deltas[h])).astype(jnp.bfloat16))
             dq_win.append(dot(dsw, kv[window, cols(h)], NN))
             for columns, low, rows in ((cols(h), dsw, q[h]), (vcols, p_win[h], scaled[h])):
-                term = dot(low, rows, TN)
+                term = across(low, rows)
                 acc[pl.ds(base, SPAN - PAIR), columns] += term[: SPAN - PAIR]
                 acc[pl.ds(base + SPAN - PAIR, PAIR), columns] = term[SPAN - PAIR :]
         dq_mem = [dot(x, k, NN) for x, k in zip(stack(ds_mem), mem_keys)]
@@ -285,14 +307,14 @@
         dright_ref[...] = finished
 
 
-def attention(slots, edges, queries, grad_out, left, own, right, table):
+def attention(regions, slots, me, queries, grad_out, left, own, right, table, size):
     rows = queries.shape[0]
     pairs = rows // PAIR
     steps = pairs + 2 * HALO // PAIR
     ext = rows + 2 * HALO
     by_pair = pl.BlockSpec((PAIR, D), lambda i, *_: (jnp.minimum(i, pairs - 1), 0))
     spec = pltpu.PrefetchScalarGridSpec(
-        num_scalar_prefetch=2,
+        num_scalar_prefetch=3,
         grid=(steps,),
         in_specs=[
             by_pair,
@@ -300,7 +322,7 @@
             pl.BlockSpec(memory_space=pl.ANY),
             pl.BlockSpec(memory_space=pl.ANY),
             pl.BlockSpec(memory_space=pl.ANY),
-            pl.BlockSpec(table.shape, lambda i, *_: (0, 0, 0), pipeline_mode=pl.Buffered(1)),
+            pl.BlockSpec(memory_space=pl.ANY),
         ],
         out_specs=[
             by_pair,
@@ -312,11 +334,12 @@
         scratch_shapes=[
             pltpu.VMEM((ext, 2 * D), jnp.bfloat16),
             pltpu.VMEM((ext, 2 * D), jnp.float32),
-            pltpu.SemaphoreType.DMA((3,)),
+            pltpu.VMEM(table.shape, table.dtype),
+            pltpu.SemaphoreType.DMA((6,)),
         ],
     )
     return pl.pallas_call(
-        functools.partial(attention_kernel, pairs=pairs),
+        functools.partial(attention_kernel, pairs=pairs, size=size),
         grid_spec=spec,
         out_shape=[
             jax.ShapeDtypeStruct((rows, D), jnp.bfloat16),
@@ -327,7 +350,7 @@
         ],
         compiler_params=pltpu.CompilerParams(vmem_limit_bytes=56 * 2**20),
         name="attention",
-    )(slots, edges, queries, grad_out, left, own, right, table)
+    )(regions, slots, me, queries, grad_out, left, own, right, table)
 
 
 def per_device(queries, keys_values, memory, block_regions, region_slot, grad_out):
@@ -341,10 +364,8 @@
     table, left, right = exchange(memory, own, size, gather)
     if not gather:
         table = lax.all_gather(memory, "seq", axis=0, tiled=True)
-    slots = region_slot[block_regions.reshape(-1)]
-    edges = jnp.stack([me == 0, me == size - 1]).astype(jnp.int32)
     attended, grad_queries, to_left, grads, to_right = attention(
-        slots, edges, queries, grad_out, left, own, right, table
+        block_regions, region_slot, me.reshape(1), queries, grad_out, left, own, right, table, size
     )
     from_right = lax.ppermute(to_left, "seq", down)
     from_left = lax.ppermute(to_right, "seq", up)

time: 112 us -> 109 us (0.973)
  Pallas kernels: 81.2 us -> 79.7 us
    pallas_call x1, Pallas kernels: 41.6 us -> 40.1 us  [attention(): pl.pallas_call(functools.partial(attention_kernel, pairs=pairs, size=size...]
    gather x1 -> x0, local copies, waits for them, and re-layouts: 1.28 us -> none  [per_device(): slots = region_slot[block_regions.reshape(-1)]]
    unnamed x4 -> x2, local copies, waits for them, and re-layouts: 6.4 us -> 6.98 us
where the time goes in v4:
time: 109 us; the launch traced here: 108 us
  Pallas kernels  79.7 us (73%)
  local copies, waits for them, and re-layouts  16.8 us (15%)
  other arithmetic  4.76 us (4%)
  starting transfers between devices  4.35 us (4%)
  waiting for transfers between devices  1.81 us (2%)
    pallas_call x1, Pallas kernels, attention(): pl.pallas_call(functools.partial(attention_kernel, pairs=pairs, size=size...  40.1 us
    pallas_call x1, Pallas kernels, exchange(): pl.pallas_call(functools.partial(exchange_kernel, size=size, gather=gathe...  39.6 us
    reshape x1, local copies, waits for them, and re-layouts, per_device(): kept = lax.optimization_barrier(grads.reshape(rows, 2, D))  7.79 us
    unnamed x2, local copies, waits for them, and re-layouts  6.98 us
    dynamic_update_slice x2, other arithmetic, per_device(): lax.dynamic_update_slice(kept, total.astype(jnp.bfloat16), (start, 0, 0))  4.76 us
    ppermute x1, starting transfers between devices, per_device(): from_right = lax.ppermute(to_left, 'seq', down)  2.43 us
  transfers between devices with their start and end apart: 2, of which 1 were waited for; matrix products, arithmetic and copies ran while one was open for 10% of the time, Pallas kernels for 0%

profile of v4, /device:TPU:1, one launch (start us, length us, event | category | flops | bytes accessed | tf_op | source)
XLA Modules:
  0.0 108.2 jit_solution(5701070247177105936)
XLA Ops:
  0.6 1.4 %copy.9.regions_ref = s32[16,4]{1,0:T(8,128)} copy(s32[16,4]{0,1:T(4,128)} %param.9) | data formatting | bytes 512 | tf_op args[3]
  2.0 5.6 %copy.10 = bf16[128,8,2,1024]{3,1,2,0:T(8,128)(2,1)} copy(bf16[128,8,2,1024]{3,2,1,0:T(2,128)(2,1)} %bitcast.5) | data formatting | bytes 8388608
  7.6 39.6 %exchange.1 = (bf16[128,64,256]{2,1,0:T(8,128)(2,1)}, bf16[128,2048]{1,0:T(8,128)(2,1)}, bf16[128,2048]{1,0:T(8,128)(2,1)}) custom-call(bf16[4,64,256]{2,1,0:T(8,128)(2,1)} %mem_ref.1, bf16[1024,2048]{1,0:T(8,128)(2,1)} %bitcast.3), custom_call_target="tpu_custom_call" | custom-call | tf_op jit(solution)/shard_map/exchange/pallas_call | solution.py:151
  47.3 40.1 %attention.1 = (bf16[1024,1024]{1,0:T(8,128)(2,1)}, bf16[1024,1024]{1,0:T(8,128)(2,1)}, bf16[128,2048]{1,0:T(8,128)(2,1)}, bf16[1024,2048]{1,0:T(8,128)(2,1)}, bf16[128,2048]{1,0:T(8,128)(2,1)}) custom-call(s32[16,4]{1,0:T(8,128)} %copy.9.regions_ref, s32[128]{0:T(128)} %slot_ref.1, s32[1]{0:T(128)} %bitcast.me_ref, bf16[1024,1024]{1,0:T(8,128)(2,1)} %q_ref.1, ...), custom_call_target="tpu_custom_call" | custom-call | tf_op jit(solution)/shard_map/attention/pallas_call | solution.py:341
  87.4 1.9 %collective-permute-start = (bf16[128,2048]{1,0:T(8,128)(2,1)}, bf16[128,2048]{1,0:T(8,128)(2,1)S(1)}, u32[]{:S(2)}, u32[]{:S(2)}) collective-permute-start(bf16[128,2048]{1,0:T(8,128)(2,1)} %get-tuple-element.17), channel_id=1, source_target_pairs={{0,1},{1,2},{2,3},{3,4},{4,5},{5,6},{6,7},{7,8},{8,9},{9,10},{10,1... | collective-permute-start | bytes 1572872 | tf_op jit(solution)/shard_map/ppermute | solution.py:371
  89.3 2.4 %collective-permute-start.1 = (bf16[128,2048]{1,0:T(8,128)(2,1)}, bf16[128,2048]{1,0:T(8,128)(2,1)S(1)}, u32[]{:S(2)}, u32[]{:S(2)}) collective-permute-start(bf16[128,2048]{1,0:T(8,128)(2,1)} %get-tuple-element.18), channel_id=1, source_target_pairs={{1,0},{2,1},{3,2},{4,3},{5,4},{6,5},{7,6},{8,7},{9,8},{10,9},{11,1... | collective-permute-start | bytes 1572872 | tf_op jit(solution)/shard_map/ppermute | solution.py:370
  91.7 7.8 %reshape.23 = bf16[1024,2,1024]{2,1,0:T(2,128)(2,1)} reshape(bf16[1024,2048]{1,0:T(8,128)(2,1)} %get-tuple-element.16) | data formatting | bytes 8388608 | tf_op jit(solution)/shard_map/reshape | solution.py:372
  99.5 1.8 %collective-permute-done = bf16[128,2048]{1,0:T(8,128)(2,1)S(1)} collective-permute-done((bf16[128,2048]{1,0:T(8,128)(2,1)}, bf16[128,2048]{1,0:T(8,128)(2,1)S(1)}, u32[]{:S(2)}, u32[]{:S(2)}) %collective-permute-start) | collective-permute-done | bytes 524320 | tf_op jit(solution)/shard_map/ppermute | solution.py:371
  101.3 1.0 reshape.24
  102.4 2.4 %fusion = bf16[1024,2,1024]{2,1,0:T(2,128)(2,1)} fusion(bf16[1024,2,1024]{2,1,0:T(2,128)(2,1)} %reshape.23, f32[128,2,1024]{2,1,0:T(2,128)S(1)} %reshape.24), kind=kLoop, calls=%fused_computation.2 | loop fusion | flops 786432 | bytes 2097152 | tf_op jit(solution)/shard_map/dynamic_update_slice | solution.py:377
  104.7 0.0 collective-permute-done.1
  104.7 1.0 reshape.25
  105.8 2.4 %fusion.1 = bf16[1024,2,1024]{2,1,0:T(2,128)(2,1)} fusion(bf16[1024,2,1024]{2,1,0:T(2,128)(2,1)} %fusion, f32[128,2,1024]{2,1,0:T(2,128)S(1)} %reshape.25), kind=kLoop, calls=%fused_computation.3 | loop fusion | flops 786432 | bytes 2097152 | tf_op jit(solution)/shard_map/dynamic_update_slice | solution.py:377
Async XLA Ops:
  87.4 14.0 %collective-permute-start = (bf16[128,2048]{1,0:T(8,128)(2,1)}, bf16[128,2048]{1,0:T(8,128)(2,1)S(1)}, u32[]{:S(2)}, u32[]{:S(2)}) collective-permute-start(bf16[128,2048]{1,0:T(8,128)(2,1)} %get-tuple-element.17), channel_id=1, source_target_pairs={{0,1},{1,2},{2,3},{3,4},{4,5},{5,6},{6,7},{7,8},{8,9},{9,10},{10,1... | collective-permute-start | bytes 1572872 | tf_op jit(solution)/shard_map/ppermute | solution.py:371
  89.3 15.5 %collective-permute-start.1 = (bf16[128,2048]{1,0:T(8,128)(2,1)}, bf16[128,2048]{1,0:T(8,128)(2,1)S(1)}, u32[]{:S(2)}, u32[]{:S(2)}) collective-permute-start(bf16[128,2048]{1,0:T(8,128)(2,1)} %get-tuple-element.18), channel_id=1, source_target_pairs={{1,0},{2,1},{3,2},{4,3},{5,4},{6,5},{7,6},{8,7},{9,8},{10,9},{11,1... | collective-permute-start | bytes 1572872 | tf_op jit(solution)/shard_map/ppermute | solution.py:370
